TPU v7x, 32 devices: a whole 2x2x4 slice. The times are simulated.
32 devices in a mesh: beam: 2 (over y), chan: 4 (over z), tgrp: 2 (over x), pol: 2 (over core).
Axes of the slice: x: 2, y: 2, z: 4, core: 2. Of those that a mesh axis runs over, the one named last changes fastest.
Arguments:
- voltages: bfloat16 [16, 8192, 512], P(('beam', 'chan', 'tgrp'), None, 'pol'), parts along dimension 0, may hold values from -6 to 6
- filter_taps: float32 [4, 8192], replicated, may hold values from -0.03125 to 0.03125
Outputs:
- visibility: float32 [512, 16, 2, 512], P('tgrp', ('beam', 'chan'), None, 'pol'), parts along dimension 1
There are 2 independent parts, one for each index of `beam`. A program takes and returns all parts, laid end to end along the dimension named above; an argument that names none is the same for every part. Nothing has to cross between parts.
All inputs are finite; a program needn't handle non-finite values.
Results may differ from a plain program's by a relative error of at most 0.013.
Values may be sent and summed in bfloat16 or wider, within the bound.
No kernel may reach another device: no remote copies, remote signals or barrier semaphores. Data moves between devices by JAX's collectives and lax.ppermute only.
A program may use at most 64 MiB of HBM per device.

v0:
```python
import math

import jax
import jax.numpy as jnp
from jax import lax
from jax.sharding import PartitionSpec as P

BAND_START = 1024
CH_DEV = 2


def passed_along(array, axis, by):
    peers = lax.axis_size(axis)
    pairs = [(i, i + by) for i in range(peers) if 0 <= i + by < peers]
    return lax.ppermute(array, axis, pairs)


def twiddle_table(length, band):
    sample = lax.broadcasted_iota(jnp.int32, (length, band), 0)
    channel = lax.broadcasted_iota(jnp.int32, (length, band), 1) + BAND_START
    angles = (sample * channel % length).astype(jnp.float32) * (2.0 * math.pi / length)
    return jnp.concatenate([jnp.cos(angles), -jnp.sin(angles)], 1)


def transform(twiddle, frame_data):
    return lax.dot_general(
        twiddle,
        frame_data,
        (((0,), (0,)), ((), ())),
        precision=lax.Precision.HIGHEST,
        preferred_element_type=jnp.float32,
    )


def body(voltages, filter_taps):
    length = voltages.shape[1]
    half_inputs = voltages.shape[2]
    tap_count = filter_taps.shape[0]
    lead_count = tap_count - 1
    band = CH_DEV * lax.axis_size("chan")
    twiddle = twiddle_table(length, band)
    own_frame = voltages[0]
    frame_wide = own_frame.astype(jnp.float32)

    def tap_term(tap_index):
        return transform(twiddle * filter_taps[tap_index][:, None], frame_wide)

    spectra = tap_term(lead_count)
    for shift_by in range(1, tap_count):
        spectra = spectra + passed_along(
            tap_term(lead_count - shift_by), ("chan", "tgrp"), shift_by
        )
    spectra = spectra.astype(jnp.bfloat16).reshape(1, 2, band, half_inputs)
    turned = lax.all_to_all(spectra, "chan", split_axis=2, concat_axis=0, tiled=True)
    gathered = lax.all_gather(turned, "pol", axis=3, tiled=True)
    inverse_count = 1.0 / (lax.axis_size("chan") * lax.axis_size("tgrp"))
    swapped = jnp.stack([gathered[:, 1], -gathered[:, 0]], 1)
    stacked = jnp.stack([gathered, swapped], 1)
    return lax.psum_scatter(
        (
            jnp.einsum("fopkc,fpkj->ckoj", stacked, turned, preferred_element_type=jnp.float32)
            * inverse_count
        ).astype(jnp.bfloat16),
        "tgrp",
        scatter_dimension=0,
        tiled=True,
    ).astype(jnp.float32)


def solution(mesh):
    return jax.shard_map(
        body,
        mesh=mesh,
        in_specs=(P(("beam", "chan", "tgrp"), None, "pol"), P()),
        out_specs=P("tgrp", ("beam", "chan"), None, "pol"),
        check_vma=False,
    )
```

profile of v0, /device:TPU:0, one launch (start us, length us, event | category | flops | bytes accessed | tf_op | source)
XLA Modules:
  0.0 72.7 jit_solution(17873396575523659024)
XLA Ops:
  6.5 0.0 reduce-scatter.2.cloned.1.call-start
  6.5 0.0 copy-start
  6.5 1.4 %fusion.50 = (f32[1,8192]{1,0:T(1,128)S(1)}, f32[1,8192]{1,0:T(1,128)S(1)}, f32[1,8192]{1,0:T(1,128)S(1)}, f32[1,8192]{1,0:T(1,128)S(1)}) fusion(f32[4,8192]{1,0:T(4,128)} %param.3), kind=kLoop, calls=%fused_computation.50 | loop fusion | bytes 262144 | tf_op jit(solution)/shard_map/slice | solution.py:46
  7.9 1.1 %fusion.39 = (f32[8192,8]{0,1:T(8,128)S(1)}, f32[8192,8]{0,1:T(8,128)S(1)}) fusion(s32[8]{0:T(128)S(1)} %iota_add_fusion), kind=kLoop, calls=%fused_computation.35 | loop fusion | flops 983040 | bytes 524320 | tf_op jit(solution)/shard_map/cos | solution.py:22
  9.0 4.0 %fusion = f32[16,256]{1,0:T(8,128)S(1)} fusion(bf16[1,8192,256]{2,1,0:T(8,128)(2,1)} %param.2, f32[8192]{0:T(1024)S(1)} %bitcast.55, f32[8192,8]{0,1:T(8,128)S(1)} %get-tuple-element.12, f32[8192,8]{0,1:T(8,128)S(1)} %get-tuple-element.11), kind=kOutput, calls=%fused_computation | convolution fusion | flops 402915328 | bytes 4767744 | tf_op jit(solution)/shard_map/dot_general | solution.py:26
  13.0 5.9 %collective-permute-start.2 = (f32[16,256]{1,0:T(8,128)S(1)}, f32[16,256]{1,0:T(8,128)S(1)}, u32[]{:S(2)}, u32[]{:S(2)}) collective-permute-start(f32[16,256]{1,0:T(8,128)S(1)} %fusion), channel_id=1, source_target_pairs={{0,6},{2,8},{4,10},{6,12},{8,14},{1,7},{3,9},{5,11},{7,13},{9,15},... | collective-permute-start | bytes 49160 | tf_op jit(solution)/shard_map/ppermute | solution.py:15
  18.9 0.0 copy-done
  18.9 1.8 %fusion.2 = f32[16,256]{1,0:T(8,128)S(1)} fusion(bf16[1,8192,256]{2,1,0:T(8,128)(2,1)S(1)} %copy-done, f32[8192]{0:T(1024)S(1)} %bitcast.54, f32[8192,8]{0,1:T(8,128)S(1)} %get-tuple-element.12, f32[8192,8]{0,1:T(8,128)S(1)} %get-tuple-element.11), kind=kOutput, calls=%fused_computation.2 | convolution fusion | flops 402915328 | bytes 4767744 | tf_op jit(solution)/shard_map/dot_general | solution.py:26
  20.7 3.5 %collective-permute-start.1 = (f32[16,256]{1,0:T(8,128)S(1)}, f32[16,256]{1,0:T(8,128)S(1)}, u32[]{:S(2)}, u32[]{:S(2)}) collective-permute-start(f32[16,256]{1,0:T(8,128)S(1)} %fusion.2), channel_id=1, source_target_pairs={{0,4},{2,6},{4,8},{6,10},{8,12},{10,14},{1,5},{3,7},{5,9},{7,11},{... | collective-permute-start | bytes 49160 | tf_op jit(solution)/shard_map/ppermute | solution.py:15
  24.2 1.8 %fusion.4 = f32[16,256]{1,0:T(8,128)S(1)} fusion(bf16[1,8192,256]{2,1,0:T(8,128)(2,1)S(1)} %copy-done, f32[8192]{0:T(1024)S(1)} %bitcast.53, f32[8192,8]{0,1:T(8,128)S(1)} %get-tuple-element.12, f32[8192,8]{0,1:T(8,128)S(1)} %get-tuple-element.11), kind=kOutput, calls=%fused_computation.4 | convolution fusion | flops 402915328 | bytes 4767744 | tf_op jit(solution)/shard_map/dot_general | solution.py:26
  25.9 3.5 %collective-permute-start = (f32[16,256]{1,0:T(8,128)S(1)}, f32[16,256]{1,0:T(8,128)S(1)}, u32[]{:S(2)}, u32[]{:S(2)}) collective-permute-start(f32[16,256]{1,0:T(8,128)S(1)} %fusion.4), channel_id=1, source_target_pairs={{0,2},{2,4},{4,6},{6,8},{8,10},{10,12},{12,14},{1,3},{3,5},{5,7},{... | collective-permute-start | bytes 49160 | tf_op jit(solution)/shard_map/ppermute | solution.py:15
  29.4 0.0 collective-permute-done.2
  29.4 0.0 collective-permute-done.1
  29.4 1.4 %collective-permute-done = f32[16,256]{1,0:T(8,128)S(1)} collective-permute-done((f32[16,256]{1,0:T(8,128)S(1)}, f32[16,256]{1,0:T(8,128)S(1)}, u32[]{:S(2)}, u32[]{:S(2)}) %collective-permute-start) | collective-permute-done | bytes 16416 | tf_op jit(solution)/shard_map/ppermute | solution.py:15
  30.8 1.8 %fusion.22 = bf16[1,2,8,256]{3,2,1,0:T(8,128)(2,1)S(1)} fusion(f32[16,256]{1,0:T(8,128)S(1)} %collective-permute-done.2, f32[16,256]{1,0:T(8,128)S(1)} %collective-permute-done.1, f32[16,256]{1,0:T(8,128)S(1)} %collective-permute-done, bf16[1,8192,256]{2,1,0:T(8,128)(2,1)S(1)} %copy-done, f32[8192]{0:T(1024)S(1)} %bitcast.52, ...), kind=kOutput, calls=%fused_computation.15 | convolution fusion | flops 402931712 | bytes 4808704 | tf_op jit(solution)/shard_map/dot_general | solution.py:26
  32.7 9.9 %all_to_all.18 = bf16[1,2,8,256]{3,1,0,2:T(2,128)(2,1)S(1)} all-to-all(bf16[1,2,8,256]{3,1,0,2:T(2,128)(2,1)S(1)} %copy.9), channel_id=1, replica_groups=mesh['beam'=2,'chan'=4,'tgrp'=2,'pol'=2] {'chan'}, dimensions={2} | all-to-all | bytes 16384 | tf_op jit(solution)/shard_map/all_to_all | solution.py:54
  42.6 1.8 %all-gather = bf16[4,1,2,2,512]{4,2,0,3,1:T(2,128)(2,1)S(1)} all-gather(bf16[4,1,2,2,256]{4,2,0,3,1:T(2,128)(2,1)S(1)} %bitcast.56), channel_id=2, replica_groups=mesh['beam'=2,'chan'=4,'tgrp'=2,'pol'=2] {'pol'}, dimensions={4}, use_global_device_ids=true | all-gather | bytes 24576 | tf_op jit(solution)/shard_map/all_gather | solution.py:55
  44.5 1.5 %fusion.9 = bf16[512,2,2,256]{0,3,2,1:T(8,128)(2,1)} fusion(bf16[4,1,2,2,512]{4,2,0,1,3:T(2,128)(2,1)S(1)} %maximum_bitcast_fusion, bf16[4,1,2,2,512]{4,2,0,1,3:T(2,128)(2,1)S(1)} %bitcast.51, bf16[1,2,4,2,256]{4,1,3,2,0:T(2,128)(2,1)S(1)} %bitcast.58), kind=kOutput, calls=%fused_computation.10 | convolution fusion | flops 9502720 | bytes 1089536 | tf_op jit(solution)/shard_map/fopkc,fpkj->ckoj/dot_general | solution.py:61
  45.9 0.0 reduce-scatter.2.cloned.1.call-update
  46.0 17.8 %reduce-scatter.2.cloned.1.call-done = bf16[256,2,2,256]{0,3,2,1:T(8,128)(2,1)} async-done(((bf16[512,2,2,256]{0,3,2,1:T(8,128)(2,1)}), bf16[256,2,2,256]{0,3,2,1:T(8,128)(2,1)}) %reduce-scatter.2.cloned.1.call-update) | async-done | bytes 524304 | tf_op jit(solution)/shard_map/reduce_scatter | solution.py:59
  63.8 2.1 %copy.12 = f32[256,2,2,256]{3,2,1,0:T(2,128)} copy(bf16[256,2,2,256]{0,3,2,1:T(8,128)(2,1)} %reduce-scatter.2.cloned.1.call-done) | data formatting | bytes 1572864 | tf_op jit(solution)/shard_map/convert_element_type | solution.py:67
  (5 shorter events, 0.1 us)
Async XLA Ops:
  6.5 57.2 %reduce-scatter.2.cloned.1.call-start = ((), (), s32[]{:S(2)}) async-start(), calls=%async_computation.2 | async-start | bytes 1572864 | tf_op jit(solution)/shard_map/reduce_scatter | solution.py:59
  6.5 12.3 %copy-start = (bf16[1,8192,256]{2,1,0:T(8,128)(2,1)S(1)}, bf16[1,8192,256]{2,1,0:T(8,128)(2,1)}, u32[]{:S(2)}) copy-start(bf16[1,8192,256]{2,1,0:T(8,128)(2,1)} %param.2) | copy-start | bytes 12582916
  13.0 16.4 %collective-permute-start.2 = (f32[16,256]{1,0:T(8,128)S(1)}, f32[16,256]{1,0:T(8,128)S(1)}, u32[]{:S(2)}, u32[]{:S(2)}) collective-permute-start(f32[16,256]{1,0:T(8,128)S(1)} %fusion), channel_id=1, source_target_pairs={{0,6},{2,8},{4,10},{6,12},{8,14},{1,7},{3,9},{5,11},{7,13},{9,15},... | collective-permute-start | bytes 49160 | tf_op jit(solution)/shard_map/ppermute | solution.py:15
  20.7 8.7 %collective-permute-start.1 = (f32[16,256]{1,0:T(8,128)S(1)}, f32[16,256]{1,0:T(8,128)S(1)}, u32[]{:S(2)}, u32[]{:S(2)}) collective-permute-start(f32[16,256]{1,0:T(8,128)S(1)} %fusion.2), channel_id=1, source_target_pairs={{0,4},{2,6},{4,8},{6,10},{8,12},{10,14},{1,5},{3,7},{5,9},{7,11},{... | collective-permute-start | bytes 49160 | tf_op jit(solution)/shard_map/ppermute | solution.py:15
  25.9 4.9 %collective-permute-start = (f32[16,256]{1,0:T(8,128)S(1)}, f32[16,256]{1,0:T(8,128)S(1)}, u32[]{:S(2)}, u32[]{:S(2)}) collective-permute-start(f32[16,256]{1,0:T(8,128)S(1)} %fusion.4), channel_id=1, source_target_pairs={{0,2},{2,4},{4,6},{6,8},{8,10},{10,12},{12,14},{1,3},{3,5},{5,7},{... | collective-permute-start | bytes 49160 | tf_op jit(solution)/shard_map/ppermute | solution.py:15
Sparse Core Ops, SparseCore 0:
  46.1 17.6 reduce-scatter.1
where the time goes:
time: 72.9 us; the launch traced here: 72.7 us
  waiting for transfers between devices  19.2 us (26%)
  between operations  13.5 us (19%)
  starting transfers between devices  12.8 us (18%)
  blocking collectives  11.7 us (16%)
  matrix products  10.8 us (15%)
  local copies, waits for them, and re-layouts  3.45 us (5%)
  other arithmetic  1.2 us (2%)
    reduce_scatter x1, waiting for transfers between devices, body(): lax.psum_scatter((jnp.einsum('fopkc,fpkj->ckoj', stacked, turned, preferr...  17.8 us
    ppermute x3, starting transfers between devices, passed_along(): return lax.ppermute(array, axis, pairs)  12.8 us
    all_to_all x1, blocking collectives, body(): lax.all_to_all(spectra, 'chan', split_axis=2, concat_axis=0, tiled=True)  9.89 us
    dot_general x4, matrix products, transform(): lax.dot_general(twiddle, frame_data, (((0,), (0,)), ((), ())), precision=...  9.35 us
    convert_element_type x1, local copies, waits for them, and re-layouts, body(): return lax.psum_scatter((jnp.einsum('fopkc,fpkj->ckoj', stacked, turned,...  2.05 us
    all_gather x1, blocking collectives, body(): gathered = lax.all_gather(turned, 'pol', axis=3, tiled=True)  1.82 us
    dot_general x1, matrix products, body(): jnp.einsum('fopkc,fpkj->ckoj', stacked, turned, preferred_element_type=jn...  1.48 us
  transfers between devices with their start and end apart: 4, of which 2 were waited for; matrix products, arithmetic and copies ran while one was open for 5% of the time, Pallas kernels for 0%

commit v1 on v0

v1 whole, which is shorter than its diff:
```python
import functools
import math

import jax
import jax.numpy as jnp
import numpy as np
from jax import lax
from jax.experimental import pallas as pl
from jax.experimental.pallas import tpu as pltpu
from jax.sharding import PartitionSpec as P

BAND_START = 1024
CH_DEV = 2
PARTS = 2
LANES = 128


def twiddle_table(length, blocks):
    channel = BAND_START + np.arange(blocks * CH_DEV, dtype=np.int64)
    phase = (channel[:, None] * np.arange(length, dtype=np.int64)) % length
    angles = phase * (2.0 * math.pi / length)
    table = np.stack([np.cos(angles), -np.sin(angles)], 0)
    table = table.reshape(PARTS, blocks, CH_DEV, length).transpose(1, 0, 2, 3)
    return table.reshape(blocks * PARTS * CH_DEV, length).astype(np.float32)


def transform_kernel(chunk, voltages_hbm, taps_ref, twiddle_hbm, out_ref, volts, table, sems):
    chunks = volts.shape[0] // chunk
    taps = taps_ref.shape[0]
    rows = table.shape[0]

    def copies(step):
        part = pl.ds(step * chunk, chunk)
        return (
            pltpu.make_async_copy(twiddle_hbm.at[:, part], table.at[:, part], sems.at[0, step]),
            pltpu.make_async_copy(voltages_hbm.at[part], volts.at[part], sems.at[1, step]),
        )

    for step in range(chunks):
        for copy in copies(step):
            copy.start()
    total = jnp.zeros((taps * rows, volts.shape[1]), jnp.float32)
    for step in range(chunks):
        part = pl.ds(step * chunk, chunk)
        table_copy, volts_copy = copies(step)
        table_copy.wait()
        turns = table[:, part]
        weights = jnp.concatenate([turns * taps_ref[t:t + 1, part] for t in range(taps)], 0)
        high = weights.astype(jnp.bfloat16)
        low = (weights - high.astype(jnp.float32)).astype(jnp.bfloat16)
        volts_copy.wait()
        both = jnp.dot(jnp.concatenate([high, low], 0), volts[part], preferred_element_type=jnp.float32)
        total = total + (both[:taps * rows] + both[taps * rows:])
    per_block = PARTS * CH_DEV
    blocks = rows // per_block
    pieces = [
        total[t * rows + b * per_block:t * rows + (b + 1) * per_block]
        for b in range(blocks)
        for t in range(taps)
    ]
    out_ref[...] = jnp.concatenate(pieces, 0).astype(out_ref.dtype)


def transform(voltages, filter_taps, twiddle):
    length, inputs = voltages.shape
    taps = filter_taps.shape[0]
    rows = twiddle.shape[0]
    chunk = min(length, 1024)
    chunks = length // chunk
    return pl.pallas_call(
        functools.partial(transform_kernel, chunk),
        out_shape=jax.ShapeDtypeStruct((taps * rows, inputs), jnp.bfloat16),
        in_specs=[
            pl.BlockSpec(memory_space=pltpu.HBM),
            pl.BlockSpec(memory_space=pltpu.VMEM),
            pl.BlockSpec(memory_space=pltpu.HBM),
        ],
        out_specs=pl.BlockSpec(memory_space=pltpu.VMEM),
        scratch_shapes=[
            pltpu.VMEM((length, inputs), jnp.bfloat16),
            pltpu.VMEM((rows, length), jnp.float32),
            pltpu.SemaphoreType.DMA((2, chunks)),
        ],
        compiler_params=pltpu.CompilerParams(vmem_limit_bytes=62 * 2**20),
        name="transform",
    )(voltages, filter_taps, twiddle)


def spectra_of(terms, taps):
    frames = terms.shape[0]
    per_tap = PARTS * CH_DEV
    spectra = []
    for frame in range(frames):
        total = None
        for tap in range(taps):
            source = frame - (taps - 1) + tap
            if source >= 0:
                term = terms[source, tap * per_tap:(tap + 1) * per_tap].astype(jnp.float32)
                total = term if total is None else total + term
        spectra.append(total.astype(jnp.bfloat16))
    return spectra


def power_kernel(taps, scale, left_ref, right_ref, out_ref):
    left = spectra_of(left_ref[...], taps)
    right = spectra_of(right_ref[...], taps)
    rows = left_ref.shape[2]
    step = 2 * CH_DEV * PARTS
    for channel in range(CH_DEV):
        a = [s[r * CH_DEV + channel:r * CH_DEV + channel + 1] for r in range(PARTS) for s in left]
        b = [s[r * CH_DEV + channel:r * CH_DEV + channel + 1] for r in range(PARTS) for s in right]
        half = len(b) // 2
        turned = [-x for x in b[half:]] + b[:half]
        a = jnp.concatenate(a, 0)
        for part, other in ((0, b), (1, turned)):
            product = scale * lax.dot_general(
                a, jnp.concatenate(other, 0), (((0,), (0,)), ((), ())), preferred_element_type=jnp.float32
            )
            for tile in range(product.shape[1] // LANES):
                start = (channel * (product.shape[1] // LANES) + tile) * PARTS + part
                out_ref[pl.ds(start, rows, stride=out_ref.shape[0] // rows), :] = product[
                    :, tile * LANES:(tile + 1) * LANES
                ]


def powers(left, right, taps, frames):
    rows, columns = left.shape[2], right.shape[2]
    tiles = columns // LANES
    out = pl.pallas_call(
        functools.partial(power_kernel, taps, 1.0 / frames),
        out_shape=jax.ShapeDtypeStruct((rows * CH_DEV * tiles * PARTS, LANES), jnp.float32),
        in_specs=[pl.BlockSpec(memory_space=pltpu.VMEM)] * 2,
        out_specs=pl.BlockSpec(memory_space=pltpu.VMEM),
        compiler_params=pltpu.CompilerParams(vmem_limit_bytes=32 * 2**20),
        name="powers",
    )(left, right)
    out = out.reshape(rows, CH_DEV, tiles, PARTS, LANES).transpose(0, 1, 3, 2, 4)
    return out.reshape(rows, CH_DEV, PARTS, columns)


def body(voltages, filter_taps):
    taps = filter_taps.shape[0]
    chans, groups = lax.axis_size("chan"), lax.axis_size("tgrp")
    frames = chans * groups
    twiddle = jnp.asarray(twiddle_table(voltages.shape[1], chans))
    terms = transform(voltages[0], filter_taps, twiddle)
    terms = terms.reshape(chans, 1, -1, terms.shape[1])
    terms = jnp.broadcast_to(terms, (chans, groups) + terms.shape[2:]).reshape((frames,) + terms.shape[2:])
    turned = lax.all_to_all(terms, ("chan", "tgrp"), split_axis=0, concat_axis=0, tiled=True)
    gathered = lax.all_gather(turned, "pol", axis=2, tiled=True)
    rows = gathered.shape[2] // groups
    left = lax.dynamic_slice_in_dim(gathered, lax.axis_index("tgrp") * rows, rows, 2)
    return powers(left, turned, taps, frames)


def solution(mesh):
    return jax.shard_map(
        body,
        mesh=mesh,
        in_specs=(P(("beam", "chan", "tgrp"), None, "pol"), P()),
        out_specs=P("tgrp", ("beam", "chan"), None, "pol"),
        check_vma=False,
    )
```

time: 72.9 us -> 23.7 us (0.33)
  between operations: 13.5 us -> 0.01 us
  waiting for transfers between devices: 19.2 us -> 6.9 us
  matrix products: 10.8 us -> 0 us
  blocking collectives: 11.7 us -> 1.89 us
  Pallas kernels: 0 us -> 6 us
  starting transfers between devices: 12.8 us -> 7.25 us
  local copies, waits for them, and re-layouts: 3.45 us -> 1.4 us
  other arithmetic: 1.2 us -> 0 us
    reduce_scatter x1 -> x0, waiting for transfers between devices: 17.8 us -> none  [body(): lax.psum_scatter((jnp.einsum('fopkc,fpkj->ckoj', stacked, turned, preferr...]
    ppermute x3 -> x0, starting transfers between devices: 12.8 us -> none  [passed_along(): return lax.ppermute(array, axis, pairs)]
    dot_general x5 -> x0, matrix products: 10.8 us -> none  [the longest x4 9.35 us: transform(): lax.dot_general(twiddle, frame_data, (((0,), (0,)), ((), ())), precision=...]
    all_to_all x1 -> x0, blocking collectives: 9.89 us -> none  [body(): lax.all_to_all(spectra, 'chan', split_axis=2, concat_axis=0, tiled=True)]
    all_to_all x0 -> x1, starting transfers between devices: none -> 7.25 us  [body(): lax.all_to_all(terms, ('chan', 'tgrp'), split_axis=0, concat_axis=0, tile...]
    all_to_all x0 -> x1, waiting for transfers between devices: none -> 6.9 us  [body(): lax.all_to_all(terms, ('chan', 'tgrp'), split_axis=0, concat_axis=0, tile...]
    pallas_call x0 -> x2, Pallas kernels: none -> 6 us  [the longest x1 4.64 us: transform(): pl.pallas_call(functools.partial(transform_kernel, chunk), out_shape=jax....]
    convert_element_type x1 -> x0, local copies, waits for them, and re-layouts: 2.05 us -> none  [body(): return lax.psum_scatter((jnp.einsum('fopkc,fpkj->ckoj', stacked, turned,...]
  transfers between devices with their start and end apart: 4 -> 1, of which waited for: 2 -> 1; matrix products, arithmetic and copies ran while one was open for 5% -> 0% of each run, Pallas kernels for 0% -> 0%
where the time goes in v1:
time: 23.7 us; the launch traced here: 23.5 us
  starting transfers between devices  7.25 us (31%)
  waiting for transfers between devices  6.9 us (29%)
  Pallas kernels  6 us (25%)
  blocking collectives  1.89 us (8%)
  local copies, waits for them, and re-layouts  1.4 us (6%)
    all_to_all x1, starting transfers between devices, body(): lax.all_to_all(terms, ('chan', 'tgrp'), split_axis=0, concat_axis=0, tile...  7.25 us
    all_to_all x1, waiting for transfers between devices, body(): lax.all_to_all(terms, ('chan', 'tgrp'), split_axis=0, concat_axis=0, tile...  6.9 us
    pallas_call x1, Pallas kernels, transform(): pl.pallas_call(functools.partial(transform_kernel, chunk), out_shape=jax....  4.64 us
    all_gather x1, blocking collectives, body(): gathered = lax.all_gather(turned, 'pol', axis=2, tiled=True)  1.89 us
    broadcast_in_dim x1, local copies, waits for them, and re-layouts, body(): jnp.broadcast_to(terms, (chans, groups) + terms.shape[2:])  1.39 us
    pallas_call x1, Pallas kernels, powers(): pl.pallas_call(functools.partial(power_kernel, taps, 1.0 / frames), out_s...  1.36 us
  transfers between devices with their start and end apart: 1, of which 1 were waited for; matrix products, arithmetic and copies ran while one was open for 0% of the time, Pallas kernels for 0%

profile of v1, /device:TPU:0, one launch (start us, length us, event | category | flops | bytes accessed | tf_op | source)
XLA Modules:
  0.0 23.5 jit_solution(2967714753480840369)
XLA Ops:
  0.0 4.6 %transform.1 = bf16[64,256]{1,0:T(8,128)(2,1)} custom-call(bf16[8192,256]{1,0:T(8,128)(2,1)} %bitcast.8, f32[4,8192]{1,0:T(4,128)} %taps_ref.1, f32[16,8192]{1,0:T(8,128)} %constant.12.clone.twiddle_hbm), custom_call_target="tpu_custom_call" | custom-call | tf_op jit(solution)/shard_map/transform/pallas_call | solution.py:70
  4.6 1.4 %broadcast_in_dim.8 = bf16[4,2,16,256]{3,2,1,0:T(8,128)(2,1)} broadcast(bf16[4,16,256]{2,1,0:T(8,128)(2,1)} %bitcast.9), dimensions={0,2,3} | broadcast | bytes 98304 | tf_op jit(solution)/shard_map/broadcast_in_dim | solution.py:148
  6.0 7.3 %all-to-all-start = ((bf16[8,16,256]{2,1,0:T(8,128)(2,1)}), bf16[8,16,256]{2,1,0:T(8,128)(2,1)S(1)}, u32[]{:S(2)}, u32[]{:S(2)}) async-start(bf16[8,16,256]{2,1,0:T(8,128)(2,1)} %bitcast.2), calls=%async_computation | async-start | bytes 131072 | tf_op jit(solution)/shard_map/all_to_all | solution.py:149
  13.3 6.9 %all-to-all-done.right_ref = bf16[8,16,256]{2,1,0:T(8,128)(2,1)S(1)} async-done(((bf16[8,16,256]{2,1,0:T(8,128)(2,1)}), bf16[8,16,256]{2,1,0:T(8,128)(2,1)S(1)}, u32[]{:S(2)}, u32[]{:S(2)}) %all-to-all-start) | async-done | bytes 65568 | tf_op jit(solution)/shard_map/all_to_all | solution.py:149
  20.2 1.9 %all_gather.3 = bf16[8,16,512]{2,1,0:T(8,128)(2,1)S(1)} all-gather(bf16[8,16,256]{2,1,0:T(8,128)(2,1)S(1)} %all-to-all-done.right_ref), channel_id=1, replica_groups=mesh['beam'=2,'chan'=4,'tgrp'=2,'pol'=2] {'pol'}, dimensions={2}, use_global_device_ids=true | all-gather | bytes 196608 | tf_op jit(solution)/shard_map/all_gather | solution.py:150
  22.1 1.4 %powers.1 = f32[2048,128]{1,0:T(8,128)} custom-call(bf16[8,16,256]{2,1,0:T(8,128)(2,1)S(1)} %constant_dynamic-slice_fusion.left_ref, bf16[8,16,256]{2,1,0:T(8,128)(2,1)S(1)} %all-to-all-done.right_ref), custom_call_target="tpu_custom_call" | custom-call | tf_op jit(solution)/shard_map/powers/pallas_call | solution.py:129
  (1 shorter events, 0.0 us)
Async XLA Ops:
  6.0 14.2 %all-to-all-start = ((bf16[8,16,256]{2,1,0:T(8,128)(2,1)}), bf16[8,16,256]{2,1,0:T(8,128)(2,1)S(1)}, u32[]{:S(2)}, u32[]{:S(2)}) async-start(bf16[8,16,256]{2,1,0:T(8,128)(2,1)} %bitcast.2), calls=%async_computation | async-start | bytes 131072 | tf_op jit(solution)/shard_map/all_to_all | solution.py:149

commit v2 on v1

v2 whole, which is shorter than its diff:
```python
import functools
import math

import jax
import jax.numpy as jnp
import numpy as np
from jax import lax
from jax.experimental import pallas as pl
from jax.experimental.pallas import tpu as pltpu
from jax.sharding import PartitionSpec as P

BAND_START = 1024
CH_DEV = 2
PARTS = 2
LANES = 128
AXES = ("chan", "tgrp", "pol")


def twiddle_table(length, blocks):
    channel = BAND_START + np.arange(blocks * CH_DEV, dtype=np.int64)
    phase = (channel[:, None] * np.arange(length, dtype=np.int64)) % length
    angles = phase * (2.0 * math.pi / length)
    table = np.stack([np.cos(angles), -np.sin(angles)], 0)
    table = table.reshape(PARTS, blocks, CH_DEV, length).transpose(1, 0, 2, 3)
    return table.reshape(blocks * PARTS * CH_DEV, length).astype(np.float32)


def transform_kernel(chunk, voltages_hbm, taps_hbm, twiddle_hbm, out_ref, volts, taps_ref, table, weights, sems):
    length = volts.shape[0]
    chunks = length // chunk
    taps = taps_ref.shape[0]
    rows = table.shape[0]
    per_block = PARTS * CH_DEV
    blocks = rows // per_block
    taps_copy = pltpu.make_async_copy(taps_hbm, taps_ref, sems.at[0])
    table_copy = pltpu.make_async_copy(twiddle_hbm, table, sems.at[1])
    taps_copy.start()
    table_copy.start()
    volts_copies = [
        pltpu.make_async_copy(
            voltages_hbm.at[pl.ds(step * chunk, chunk)], volts.at[pl.ds(step * chunk, chunk)], sems.at[2 + step]
        )
        for step in range(chunks)
    ]
    for copy in volts_copies:
        copy.start()
    taps_copy.wait()
    table_copy.wait()
    for step in range(chunks):
        part = pl.ds(step * chunk, chunk)
        turns = table[:, part]
        for t in range(taps):
            exact = turns * taps_ref[t:t + 1, part]
            high = exact.astype(jnp.bfloat16)
            weights[t * rows:(t + 1) * rows, part] = high
            weights[(taps + t) * rows:(taps + t + 1) * rows, part] = (
                exact - high.astype(jnp.float32)
            ).astype(jnp.bfloat16)
    total = jnp.zeros((2 * taps * rows, volts.shape[1]), jnp.float32)
    for step in range(chunks):
        part = pl.ds(step * chunk, chunk)
        volts_copies[step].wait()
        total = total + jnp.dot(weights[:, part], volts[part], preferred_element_type=jnp.float32)
    total = total[:taps * rows] + total[taps * rows:]
    mine = lax.axis_index("chan")
    for block in range(blocks):
        pieces = [
            total[t * rows + block * per_block:t * rows + (block + 1) * per_block] for t in range(taps)
        ]
        out_ref[lax.bitwise_xor(mine, block)] = jnp.concatenate(pieces, 0).astype(out_ref.dtype)


def transform(voltages, filter_taps, twiddle):
    length, inputs = voltages.shape
    taps = filter_taps.shape[0]
    rows = twiddle.shape[0]
    chunk = min(length, 1024)
    chunks = length // chunk
    per_block = PARTS * CH_DEV
    return pl.pallas_call(
        functools.partial(transform_kernel, chunk),
        out_shape=jax.ShapeDtypeStruct((rows // per_block, taps * per_block, inputs), jnp.bfloat16),
        in_specs=[pl.BlockSpec(memory_space=pltpu.HBM)] * 3,
        out_specs=pl.BlockSpec(memory_space=pltpu.VMEM),
        scratch_shapes=[
            pltpu.VMEM((length, inputs), jnp.bfloat16),
            pltpu.VMEM((taps, length), jnp.float32),
            pltpu.VMEM((rows, length), jnp.float32),
            pltpu.VMEM((2 * taps * rows, length), jnp.bfloat16),
            pltpu.SemaphoreType.DMA((2 + chunks,)),
        ],
        compiler_params=pltpu.CompilerParams(vmem_limit_bytes=int(53.8 * 2**20)),
        name="transform",
    )(voltages, filter_taps, twiddle)


def moved(array, frame_bits, swap):
    chans, groups = lax.axis_size("chan"), lax.axis_size("tgrp")
    count = chans * groups * 2
    return lax.ppermute(array, AXES, [(i, i ^ (frame_bits * 2 + swap)) for i in range(count)])


def exchanged(terms):
    chans, groups = lax.axis_size("chan"), lax.axis_size("tgrp")
    held = {(0, 0): terms}
    bits = [groups << b for b in reversed(range(chans.bit_length() - 1))]
    bits += [1 << b for b in reversed(range(groups.bit_length() - 1))]
    for bit in bits:
        if bit >= groups:
            keep = bit // groups
            sent = {key: value[keep:] for key, value in held.items()}
            held = {key: value[:keep] for key, value in held.items()}
        else:
            sent = dict(held)
        keys = list(sent)
        single = [key for key in keys if (key[0], 1 - key[1]) not in sent]
        got = moved(jnp.concatenate([sent[key] for key in keys], 0), bit, 1)
        other = moved(jnp.concatenate([held[key] for key in single], 0), 0, 1)
        depth = held[keys[0]].shape[0]
        for index, (frame, half) in enumerate(keys):
            held[frame ^ bit, 1 - half] = got[index * depth:(index + 1) * depth]
        for index, (frame, half) in enumerate(single):
            held[frame, 1 - half] = other[index * depth:(index + 1) * depth]
    single = [key for key in held if (key[0], 1 - key[1]) not in held]
    other = moved(jnp.concatenate([held[key] for key in single], 0), 0, 1)
    for index, (frame, half) in enumerate(single):
        held[frame, 1 - half] = other[index:index + 1]
    return held


def power_kernel(taps, groups, scale, order, *refs):
    piece_refs, out_ref, terms = refs[:-2], refs[-2], refs[-1]
    frames, columns = terms.shape[1], terms.shape[3]
    per_tap = PARTS * CH_DEV
    tiles = columns // LANES
    for (frame, half), ref in zip(order, piece_refs):
        terms[half, frame] = ref[0]
    group = lax.axis_index("tgrp")
    mine = lax.axis_index("chan") * groups + group
    rows = 2 * columns // groups
    left_start = group * rows
    left_half = lax.bitwise_xor(left_start // columns, lax.axis_index("pol"))

    def spectra_of(half):
        loaded = [terms[half, lax.bitwise_xor(mine, frame)].astype(jnp.float32) for frame in range(frames)]
        spectra = []
        for frame in range(frames):
            total = None
            for tap in range(taps):
                source = frame - (taps - 1) + tap
                if source >= 0:
                    term = loaded[source][tap * per_tap:(tap + 1) * per_tap]
                    total = term if total is None else total + term
            spectra.append(total)
        return spectra

    left = jnp.concatenate(spectra_of(left_half), 0)
    if rows != columns:
        left = pltpu.roll(left, columns - left_start % columns, 1)[:, :rows]
    right = spectra_of(0)
    turned = jnp.concatenate([x for s in right for x in (-s[CH_DEV:], s[:CH_DEV])], 0)
    right = jnp.concatenate(right, 0)
    channel_of = lax.broadcasted_iota(jnp.int32, right.shape, 0) % CH_DEV
    against = jnp.concatenate(
        [
            jnp.where(channel_of == channel, x, 0.0)[:, tile * LANES:(tile + 1) * LANES]
            for channel in range(CH_DEV)
            for tile in range(tiles)
            for x in (right, turned)
        ],
        1,
    ).astype(jnp.bfloat16)
    product = scale * lax.dot_general(
        left.astype(jnp.bfloat16), against, (((0,), (0,)), ((), ())), preferred_element_type=jnp.float32
    )
    per_row = CH_DEV * tiles * PARTS
    for index in range(per_row):
        out_ref[pl.ds(index, rows, stride=per_row), :] = product[:, index * LANES:(index + 1) * LANES]


def powers(held, taps):
    groups = lax.axis_size("tgrp")
    order = sorted(held)
    frames = len(order) // 2
    _, depth, columns = held[order[0]].shape
    rows = 2 * columns // groups
    tiles = columns // LANES
    out = pl.pallas_call(
        functools.partial(power_kernel, taps, groups, 1.0 / frames, order),
        out_shape=jax.ShapeDtypeStruct((rows * CH_DEV * tiles * PARTS, LANES), jnp.float32),
        in_specs=[pl.BlockSpec(memory_space=pltpu.VMEM)] * len(order),
        out_specs=pl.BlockSpec(memory_space=pltpu.VMEM),
        scratch_shapes=[pltpu.VMEM((2, frames, depth, columns), jnp.bfloat16)],
        compiler_params=pltpu.CompilerParams(vmem_limit_bytes=32 * 2**20),
        name="powers",
    )(*[held[key] for key in order])
    out = out.reshape(rows, CH_DEV, tiles, PARTS, LANES).transpose(0, 1, 3, 2, 4)
    return out.reshape(rows, CH_DEV, PARTS, columns)


def body(voltages, filter_taps):
    twiddle = jnp.asarray(twiddle_table(voltages.shape[1], lax.axis_size("chan")))
    terms = transform(voltages[0], filter_taps, twiddle)
    return powers(exchanged(terms), filter_taps.shape[0])


def solution(mesh):
    return jax.shard_map(
        body,
        mesh=mesh,
        in_specs=(P(("beam", "chan", "tgrp"), None, "pol"), P()),
        out_specs=P("tgrp", ("beam", "chan"), None, "pol"),
        check_vma=False,
    )
```

time: 23.7 us -> 18.1 us (0.76)
  waiting for transfers between devices: 6.9 us -> 4.4 us
  blocking collectives: 1.89 us -> 0 us
  starting transfers between devices: 7.25 us -> 9.06 us
  Pallas kernels: 6 us -> 4.43 us
  local copies, waits for them, and re-layouts: 1.4 us -> 0.02 us
    ppermute x0 -> x7, starting transfers between devices: none -> 9.06 us  [moved(): lax.ppermute(array, AXES, [(i, i ^ frame_bits * 2 + swap) for i in range(...]
    all_to_all x1 -> x0, starting transfers between devices: 7.25 us -> none  [body(): lax.all_to_all(terms, ('chan', 'tgrp'), split_axis=0, concat_axis=0, tile...]
    all_to_all x1 -> x0, waiting for transfers between devices: 6.9 us -> none  [body(): lax.all_to_all(terms, ('chan', 'tgrp'), split_axis=0, concat_axis=0, tile...]
    ppermute x0 -> x7, waiting for transfers between devices: none -> 4.4 us  [moved(): lax.ppermute(array, AXES, [(i, i ^ frame_bits * 2 + swap) for i in range(...]
    all_gather x1 -> x0, blocking collectives: 1.89 us -> none  [body(): gathered = lax.all_gather(turned, 'pol', axis=2, tiled=True)]
    pallas_call x1, Pallas kernels: 4.64 us -> 3.07 us  [transform(): pl.pallas_call(functools.partial(transform_kernel, chunk), out_shape=jax....]
    broadcast_in_dim x1 -> x0, local copies, waits for them, and re-layouts: 1.39 us -> none  [body(): jnp.broadcast_to(terms, (chans, groups) + terms.shape[2:])]
  transfers between devices with their start and end apart: 1 -> 7, of which waited for: 1 -> 5; matrix products, arithmetic and copies ran while one was open for 0% -> 0% of each run, Pallas kernels for 0% -> 0%
where the time goes in v2:
time: 18.1 us; the launch traced here: 18 us
  starting transfers between devices  9.06 us (50%)
  Pallas kernels  4.43 us (24%)
  waiting for transfers between devices  4.4 us (24%)
    ppermute x7, starting transfers between devices, moved(): lax.ppermute(array, AXES, [(i, i ^ frame_bits * 2 + swap) for i in range(...  9.06 us
    ppermute x7, waiting for transfers between devices, moved(): lax.ppermute(array, AXES, [(i, i ^ frame_bits * 2 + swap) for i in range(...  4.4 us
    pallas_call x1, Pallas kernels, transform(): pl.pallas_call(functools.partial(transform_kernel, chunk), out_shape=jax....  3.07 us
    pallas_call x1, Pallas kernels, powers(): pl.pallas_call(functools.partial(power_kernel, taps, groups, 1.0 / frames...  1.36 us
  transfers between devices with their start and end apart: 7, of which 5 were waited for; matrix products, arithmetic and copies ran while one was open for 0% of the time, Pallas kernels for 0%

profile of v2, /device:TPU:0, one launch (start us, length us, event | category | flops | bytes accessed | tf_op | source)
XLA Modules:
  0.0 18.0 jit_solution(14637367422964757504)
XLA Ops:
  0.0 3.1 %transform.1 = bf16[4,16,256]{2,1,0:T(8,128)(2,1)S(1)} custom-call(bf16[8192,256]{1,0:T(8,128)(2,1)} %bitcast.6, f32[4,8192]{1,0:T(4,128)} %taps_hbm.1, f32[16,8192]{1,0:T(8,128)} %constant.2.clone.twiddle_hbm), custom_call_target="tpu_custom_call" | custom-call | tf_op jit(solution)/shard_map/transform/pallas_call | solution.py:80
  3.1 3.5 %collective-permute-start.1 = (bf16[2,16,256]{2,1,0:T(8,128)(2,1)S(1)}, bf16[2,16,256]{2,1,0:T(8,128)(2,1)S(1)}, u32[]{:S(2)}, u32[]{:S(2)}) collective-permute-start(bf16[2,16,256]{2,1,0:T(8,128)(2,1)S(1)} %get-tuple-element.15), channel_id=1, source_target_pairs={{0,9},{1,8},{2,11},{3,10},{4,13},{5,12},{6,15},{7,14},{8,1},{9,0},... | collective-permute-start | bytes 49160 | tf_op jit(solution)/shard_map/ppermute | solution.py:100
  6.6 0.7 %collective-permute-start = (bf16[2,16,256]{2,1,0:T(8,128)(2,1)S(1)}, bf16[2,16,256]{2,1,0:T(8,128)(2,1)S(1)}, u32[]{:S(2)}, u32[]{:S(2)}) collective-permute-start(bf16[2,16,256]{2,1,0:T(8,128)(2,1)S(1)} %get-tuple-element.16), channel_id=1, source_target_pairs={{0,1},{1,0},{2,3},{3,2},{4,5},{5,4},{6,7},{7,6},{8,9},{9,8},{10,11... | collective-permute-start | bytes 49160 | tf_op jit(solution)/shard_map/ppermute | solution.py:100
  7.3 0.8 %collective-permute-done.1 = bf16[2,16,256]{2,1,0:T(8,128)(2,1)S(1)} collective-permute-done((bf16[2,16,256]{2,1,0:T(8,128)(2,1)S(1)}, bf16[2,16,256]{2,1,0:T(8,128)(2,1)S(1)}, u32[]{:S(2)}, u32[]{:S(2)}) %collective-permute-start.1) | collective-permute-done | bytes 16416 | tf_op jit(solution)/shard_map/ppermute | solution.py:100
  8.1 0.1 collective-permute-done
  8.2 1.9 %collective-permute-start.2 = (bf16[3,16,256]{2,1,0:T(8,128)(2,1)S(1)}, bf16[3,16,256]{2,1,0:T(8,128)(2,1)S(1)}, u32[]{:S(2)}, u32[]{:S(2)}) collective-permute-start(bf16[3,16,256]{2,1,0:T(8,128)(2,1)S(1)} %pad_maximum_fusion), channel_id=1, source_target_pairs={{0,5},{1,4},{2,7},{3,6},{4,1},{5,0},{6,3},{7,2},{8,13},{9,12},{10,... | collective-permute-start | bytes 73736 | tf_op jit(solution)/shard_map/ppermute | solution.py:100
  10.1 0.4 %collective-permute-start.3 = (bf16[1,16,256]{2,1,0:T(8,128)(2,1)S(1)}, bf16[1,16,256]{2,1,0:T(8,128)(2,1)S(1)}, u32[]{:S(2)}, u32[]{:S(2)}) collective-permute-start(bf16[1,16,256]{2,1,0:T(8,128)(2,1)S(1)} %get-tuple-element.20.refs_9_), channel_id=1, source_target_pairs={{0,1},{1,0},{2,3},{3,2},{4,5},{5,4},{6,7},{7,6},{8,9},{9,8},{10,11... | collective-permute-start | bytes 24584 | tf_op jit(solution)/shard_map/ppermute | solution.py:100
  10.5 1.1 %collective-permute-done.2 = bf16[3,16,256]{2,1,0:T(8,128)(2,1)S(1)} collective-permute-done((bf16[3,16,256]{2,1,0:T(8,128)(2,1)S(1)}, bf16[3,16,256]{2,1,0:T(8,128)(2,1)S(1)}, u32[]{:S(2)}, u32[]{:S(2)}) %collective-permute-start.2) | collective-permute-done | bytes 24608 | tf_op jit(solution)/shard_map/ppermute | solution.py:100
  11.6 0.0 collective-permute-done.3.refs_8_
  11.6 1.7 %collective-permute-start.4 = (bf16[7,16,256]{2,1,0:T(8,128)(2,1)S(1)}, bf16[7,16,256]{2,1,0:T(8,128)(2,1)S(1)}, u32[]{:S(2)}, u32[]{:S(2)}) collective-permute-start(bf16[7,16,256]{2,1,0:T(8,128)(2,1)S(1)} %constant_dynamic-update-slice_fusion), channel_id=1, source_target_pairs={{0,3},{1,2},{2,1},{3,0},{4,7},{5,6},{6,5},{7,4},{8,11},{9,10},{10,... | collective-permute-start | bytes 172040 | tf_op jit(solution)/shard_map/ppermute | solution.py:100
  13.3 0.4 %collective-permute-start.5 = (bf16[1,16,256]{2,1,0:T(8,128)(2,1)S(1)}, bf16[1,16,256]{2,1,0:T(8,128)(2,1)S(1)}, u32[]{:S(2)}, u32[]{:S(2)}) collective-permute-start(bf16[1,16,256]{2,1,0:T(8,128)(2,1)S(1)} %get-tuple-element.17.refs_12_), channel_id=1, source_target_pairs={{0,1},{1,0},{2,3},{3,2},{4,5},{5,4},{6,7},{7,6},{8,9},{9,8},{10,11... | collective-permute-start | bytes 24584 | tf_op jit(solution)/shard_map/ppermute | solution.py:100
  13.7 1.6 %collective-permute-done.4 = bf16[7,16,256]{2,1,0:T(8,128)(2,1)S(1)} collective-permute-done((bf16[7,16,256]{2,1,0:T(8,128)(2,1)S(1)}, bf16[7,16,256]{2,1,0:T(8,128)(2,1)S(1)}, u32[]{:S(2)}, u32[]{:S(2)}) %collective-permute-start.4) | collective-permute-done | bytes 57376 | tf_op jit(solution)/shard_map/ppermute | solution.py:100
  15.3 0.4 %collective-permute-start.6 = (bf16[1,16,256]{2,1,0:T(8,128)(2,1)S(1)}, bf16[1,16,256]{2,1,0:T(8,128)(2,1)S(1)}, u32[]{:S(2)}, u32[]{:S(2)}) collective-permute-start(bf16[1,16,256]{2,1,0:T(8,128)(2,1)S(1)} %get-tuple-element.5.refs_15_), channel_id=1, source_target_pairs={{0,1},{1,0},{2,3},{3,2},{4,5},{5,4},{6,7},{7,6},{8,9},{9,8},{10,11... | collective-permute-start | bytes 24584 | tf_op jit(solution)/shard_map/ppermute | solution.py:100
  15.8 0.0 collective-permute-done.5.refs_13_
  15.8 0.8 %collective-permute-done.6.refs_14_ = bf16[1,16,256]{2,1,0:T(8,128)(2,1)S(1)} collective-permute-done((bf16[1,16,256]{2,1,0:T(8,128)(2,1)S(1)}, bf16[1,16,256]{2,1,0:T(8,128)(2,1)S(1)}, u32[]{:S(2)}, u32[]{:S(2)}) %collective-permute-start.6) | collective-permute-done | bytes 8224 | tf_op jit(solution)/shard_map/ppermute | solution.py:100
  16.6 1.4 %powers.1 = f32[2048,128]{1,0:T(8,128)} custom-call(bf16[1,16,256]{2,1,0:T(8,128)(2,1)S(1)} %get-tuple-element.14.refs_0_, bf16[1,16,256]{2,1,0:T(8,128)(2,1)S(1)} %get-tuple-element.25.refs_1_, bf16[1,16,256]{2,1,0:T(8,128)(2,1)S(1)} %get-tuple-element.11.refs_2_, bf16[1,16,256]{2,1,0:T(8,128)(2,1)S(1)} %get-tuple-element.10.refs_3_, ...), custom_call_target="tpu_custom_call" | custom-call | tf_op jit(solution)/shard_map/powers/pallas_call | solution.py:188
  (9 shorter events, 0.0 us)
Async XLA Ops:
  3.1 5.0 %collective-permute-start.1 = (bf16[2,16,256]{2,1,0:T(8,128)(2,1)S(1)}, bf16[2,16,256]{2,1,0:T(8,128)(2,1)S(1)}, u32[]{:S(2)}, u32[]{:S(2)}) collective-permute-start(bf16[2,16,256]{2,1,0:T(8,128)(2,1)S(1)} %get-tuple-element.15), channel_id=1, source_target_pairs={{0,9},{1,8},{2,11},{3,10},{4,13},{5,12},{6,15},{7,14},{8,1},{9,0},... | collective-permute-start | bytes 49160 | tf_op jit(solution)/shard_map/ppermute | solution.py:100
  6.6 1.5 %collective-permute-start = (bf16[2,16,256]{2,1,0:T(8,128)(2,1)S(1)}, bf16[2,16,256]{2,1,0:T(8,128)(2,1)S(1)}, u32[]{:S(2)}, u32[]{:S(2)}) collective-permute-start(bf16[2,16,256]{2,1,0:T(8,128)(2,1)S(1)} %get-tuple-element.16), channel_id=1, source_target_pairs={{0,1},{1,0},{2,3},{3,2},{4,5},{5,4},{6,7},{7,6},{8,9},{9,8},{10,11... | collective-permute-start | bytes 49160 | tf_op jit(solution)/shard_map/ppermute | solution.py:100
  8.2 3.4 %collective-permute-start.2 = (bf16[3,16,256]{2,1,0:T(8,128)(2,1)S(1)}, bf16[3,16,256]{2,1,0:T(8,128)(2,1)S(1)}, u32[]{:S(2)}, u32[]{:S(2)}) collective-permute-start(bf16[3,16,256]{2,1,0:T(8,128)(2,1)S(1)} %pad_maximum_fusion), channel_id=1, source_target_pairs={{0,5},{1,4},{2,7},{3,6},{4,1},{5,0},{6,3},{7,2},{8,13},{9,12},{10,... | collective-permute-start | bytes 73736 | tf_op jit(solution)/shard_map/ppermute | solution.py:100
  10.1 1.5 %collective-permute-start.3 = (bf16[1,16,256]{2,1,0:T(8,128)(2,1)S(1)}, bf16[1,16,256]{2,1,0:T(8,128)(2,1)S(1)}, u32[]{:S(2)}, u32[]{:S(2)}) collective-permute-start(bf16[1,16,256]{2,1,0:T(8,128)(2,1)S(1)} %get-tuple-element.20.refs_9_), channel_id=1, source_target_pairs={{0,1},{1,0},{2,3},{3,2},{4,5},{5,4},{6,7},{7,6},{8,9},{9,8},{10,11... | collective-permute-start | bytes 24584 | tf_op jit(solution)/shard_map/ppermute | solution.py:100
  11.6 3.7 %collective-permute-start.4 = (bf16[7,16,256]{2,1,0:T(8,128)(2,1)S(1)}, bf16[7,16,256]{2,1,0:T(8,128)(2,1)S(1)}, u32[]{:S(2)}, u32[]{:S(2)}) collective-permute-start(bf16[7,16,256]{2,1,0:T(8,128)(2,1)S(1)} %constant_dynamic-update-slice_fusion), channel_id=1, source_target_pairs={{0,3},{1,2},{2,1},{3,0},{4,7},{5,6},{6,5},{7,4},{8,11},{9,10},{10,... | collective-permute-start | bytes 172040 | tf_op jit(solution)/shard_map/ppermute | solution.py:100
  13.3 2.5 %collective-permute-start.5 = (bf16[1,16,256]{2,1,0:T(8,128)(2,1)S(1)}, bf16[1,16,256]{2,1,0:T(8,128)(2,1)S(1)}, u32[]{:S(2)}, u32[]{:S(2)}) collective-permute-start(bf16[1,16,256]{2,1,0:T(8,128)(2,1)S(1)} %get-tuple-element.17.refs_12_), channel_id=1, source_target_pairs={{0,1},{1,0},{2,3},{3,2},{4,5},{5,4},{6,7},{7,6},{8,9},{9,8},{10,11... | collective-permute-start | bytes 24584 | tf_op jit(solution)/shard_map/ppermute | solution.py:100
  15.3 1.3 %collective-permute-start.6 = (bf16[1,16,256]{2,1,0:T(8,128)(2,1)S(1)}, bf16[1,16,256]{2,1,0:T(8,128)(2,1)S(1)}, u32[]{:S(2)}, u32[]{:S(2)}) collective-permute-start(bf16[1,16,256]{2,1,0:T(8,128)(2,1)S(1)} %get-tuple-element.5.refs_15_), channel_id=1, source_target_pairs={{0,1},{1,0},{2,3},{3,2},{4,5},{5,4},{6,7},{7,6},{8,9},{9,8},{10,11... | collective-permute-start | bytes 24584 | tf_op jit(solution)/shard_map/ppermute | solution.py:100

commit v3 on v2

--- a/solution.py
+++ b/solution.py
@@ -102,39 +102,37 @@
 
 def exchanged(terms):
     chans, groups = lax.axis_size("chan"), lax.axis_size("tgrp")
-    held = {(0, 0): terms}
+    held = {0: (terms, 0)}
     bits = [groups << b for b in reversed(range(chans.bit_length() - 1))]
     bits += [1 << b for b in reversed(range(groups.bit_length() - 1))]
-    for bit in bits:
-        if bit >= groups:
-            keep = bit // groups
-            sent = {key: value[keep:] for key, value in held.items()}
-            held = {key: value[:keep] for key, value in held.items()}
-        else:
-            sent = dict(held)
-        keys = list(sent)
-        single = [key for key in keys if (key[0], 1 - key[1]) not in sent]
-        got = moved(jnp.concatenate([sent[key] for key in keys], 0), bit, 1)
-        other = moved(jnp.concatenate([held[key] for key in single], 0), 0, 1)
-        depth = held[keys[0]].shape[0]
-        for index, (frame, half) in enumerate(keys):
-            held[frame ^ bit, 1 - half] = got[index * depth:(index + 1) * depth]
-        for index, (frame, half) in enumerate(single):
-            held[frame, 1 - half] = other[index * depth:(index + 1) * depth]
-    single = [key for key in held if (key[0], 1 - key[1]) not in held]
-    other = moved(jnp.concatenate([held[key] for key in single], 0), 0, 1)
-    for index, (frame, half) in enumerate(single):
-        held[frame, 1 - half] = other[index:index + 1]
-    return held
-
-
-def power_kernel(taps, groups, scale, order, *refs):
-    piece_refs, out_ref, terms = refs[:-2], refs[-2], refs[-1]
+    rounds = [bits[:len(bits) % 2]] + [bits[i:i + 2] for i in range(len(bits) % 2, len(bits), 2)]
+    for bits in rounds:
+        of_chan = [bit for bit in bits if bit >= groups]
+
+        def blocks_for(value, mask):
+            count = value.shape[0] >> len(of_chan)
+            index = sum(1 << i for i, bit in enumerate(reversed(of_chan)) if mask & bit)
+            return value[index * count:(index + 1) * count]
+
+        kept = {frame: (blocks_for(value, 0), half) for frame, (value, half) in held.items()}
+        masks = [sum(bit for i, bit in enumerate(bits) if pick >> i & 1) for pick in range(1, 1 << len(bits))]
+        for mask in reversed(masks):
+            got = moved(jnp.concatenate([blocks_for(value, mask) for value, _ in held.values()], 0), mask, 1)
+            count = got.shape[0] // len(held)
+            for index, (frame, (_, half)) in enumerate(held.items()):
+                kept[frame ^ mask] = (got[index * count:(index + 1) * count], 1 - half)
+        held = kept
+    order = sorted(held)
+    return jnp.concatenate([held[frame][0] for frame in order], 0), [held[frame][1] for frame in order]
+
+
+def power_kernel(taps, groups, scale, halves, had_ref, got_ref, out_ref, terms):
     frames, columns = terms.shape[1], terms.shape[3]
     per_tap = PARTS * CH_DEV
     tiles = columns // LANES
-    for (frame, half), ref in zip(order, piece_refs):
-        terms[half, frame] = ref[0]
+    for frame, half in enumerate(halves):
+        terms[half, frame] = had_ref[frame]
+        terms[1 - half, frame] = got_ref[frame]
     group = lax.axis_index("tgrp")
     mine = lax.axis_index("chan") * groups + group
     rows = 2 * columns // groups
@@ -178,22 +176,20 @@
         out_ref[pl.ds(index, rows, stride=per_row), :] = product[:, index * LANES:(index + 1) * LANES]
 
 
-def powers(held, taps):
+def powers(had, halves, taps):
     groups = lax.axis_size("tgrp")
-    order = sorted(held)
-    frames = len(order) // 2
-    _, depth, columns = held[order[0]].shape
+    frames, depth, columns = had.shape
     rows = 2 * columns // groups
     tiles = columns // LANES
     out = pl.pallas_call(
-        functools.partial(power_kernel, taps, groups, 1.0 / frames, order),
+        functools.partial(power_kernel, taps, groups, 1.0 / frames, halves),
         out_shape=jax.ShapeDtypeStruct((rows * CH_DEV * tiles * PARTS, LANES), jnp.float32),
-        in_specs=[pl.BlockSpec(memory_space=pltpu.VMEM)] * len(order),
+        in_specs=[pl.BlockSpec(memory_space=pltpu.VMEM)] * 2,
         out_specs=pl.BlockSpec(memory_space=pltpu.VMEM),
         scratch_shapes=[pltpu.VMEM((2, frames, depth, columns), jnp.bfloat16)],
         compiler_params=pltpu.CompilerParams(vmem_limit_bytes=32 * 2**20),
         name="powers",
-    )(*[held[key] for key in order])
+    )(had, moved(had, 0, 1))
     out = out.reshape(rows, CH_DEV, tiles, PARTS, LANES).transpose(0, 1, 3, 2, 4)
     return out.reshape(rows, CH_DEV, PARTS, columns)
 
@@ -201,7 +197,8 @@
 def body(voltages, filter_taps):
     twiddle = jnp.asarray(twiddle_table(voltages.shape[1], lax.axis_size("chan")))
     terms = transform(voltages[0], filter_taps, twiddle)
-    return powers(exchanged(terms), filter_taps.shape[0])
+    had, halves = exchanged(terms)
+    return powers(had, halves, filter_taps.shape[0])
 
 
 def solution(mesh):

time: 18.1 us -> 17.5 us (0.967)
  starting transfers between devices: 9.06 us -> 7.19 us
  waiting for transfers between devices: 4.4 us -> 5.66 us
    ppermute x7 -> x5, starting transfers between devices: 9.06 us -> 7.19 us  [moved(): lax.ppermute(array, AXES, [(i, i ^ frame_bits * 2 + swap) for i in range(...]
    ppermute x7 -> x5, waiting for transfers between devices: 4.4 us -> 5.66 us  [moved(): lax.ppermute(array, AXES, [(i, i ^ frame_bits * 2 + swap) for i in range(...]
  transfers between devices with their start and end apart: 7 -> 5, of which waited for: 5 -> 3; matrix products, arithmetic and copies ran while one was open for 0% -> 0% of each run, Pallas kernels for 0% -> 0%
where the time goes in v3:
time: 17.5 us; the launch traced here: 17.4 us
  starting transfers between devices  7.19 us (41%)
  waiting for transfers between devices  5.66 us (32%)
  Pallas kernels  4.44 us (25%)
    ppermute x5, starting transfers between devices, moved(): lax.ppermute(array, AXES, [(i, i ^ frame_bits * 2 + swap) for i in range(...  7.19 us
    ppermute x5, waiting for transfers between devices, moved(): lax.ppermute(array, AXES, [(i, i ^ frame_bits * 2 + swap) for i in range(...  5.66 us
    pallas_call x1, Pallas kernels, transform(): pl.pallas_call(functools.partial(transform_kernel, chunk), out_shape=jax....  3.07 us
    pallas_call x1, Pallas kernels, powers(): pl.pallas_call(functools.partial(power_kernel, taps, groups, 1.0 / frames...  1.37 us
  transfers between devices with their start and end apart: 5, of which 3 were waited for; matrix products, arithmetic and copies ran while one was open for 0% of the time, Pallas kernels for 0%

profile of v3, /device:TPU:0, one launch (start us, length us, event | category | flops | bytes accessed | tf_op | source)
XLA Modules:
  0.0 17.4 jit_solution(6581480502715224846)
XLA Ops:
  0.0 3.1 %transform.1 = bf16[4,16,256]{2,1,0:T(8,128)(2,1)S(1)} custom-call(bf16[8192,256]{1,0:T(8,128)(2,1)} %bitcast.6, f32[4,8192]{1,0:T(4,128)} %taps_hbm.1, f32[16,8192]{1,0:T(8,128)} %constant.2.clone.twiddle_hbm), custom_call_target="tpu_custom_call" | custom-call | tf_op jit(solution)/shard_map/transform/pallas_call | solution.py:80
  3.1 3.5 %collective-permute-start = (bf16[2,16,256]{2,1,0:T(8,128)(2,1)S(1)}, bf16[2,16,256]{2,1,0:T(8,128)(2,1)S(1)}, u32[]{:S(2)}, u32[]{:S(2)}) collective-permute-start(bf16[2,16,256]{2,1,0:T(8,128)(2,1)S(1)} %slice.52), channel_id=1, source_target_pairs={{0,9},{1,8},{2,11},{3,10},{4,13},{5,12},{6,15},{7,14},{8,1},{9,0},... | collective-permute-start | bytes 49160 | tf_op jit(solution)/shard_map/ppermute | solution.py:100
  6.6 1.4 %collective-permute-done = bf16[2,16,256]{2,1,0:T(8,128)(2,1)S(1)} collective-permute-done((bf16[2,16,256]{2,1,0:T(8,128)(2,1)S(1)}, bf16[2,16,256]{2,1,0:T(8,128)(2,1)S(1)}, u32[]{:S(2)}, u32[]{:S(2)}) %collective-permute-start) | collective-permute-done | bytes 16416 | tf_op jit(solution)/shard_map/ppermute | solution.py:100
  8.1 1.8 %collective-permute-start.1 = (bf16[2,16,256]{2,1,0:T(8,128)(2,1)S(1)}, bf16[2,16,256]{2,1,0:T(8,128)(2,1)S(1)}, u32[]{:S(2)}, u32[]{:S(2)}) collective-permute-start(bf16[2,16,256]{2,1,0:T(8,128)(2,1)S(1)} %pad_maximum_fusion), channel_id=1, source_target_pairs={{0,3},{1,2},{2,1},{3,0},{4,7},{5,6},{6,5},{7,4},{8,11},{9,10},{10,... | collective-permute-start | bytes 49160 | tf_op jit(solution)/shard_map/ppermute | solution.py:100
  9.9 1.6 %collective-permute-start.3 = (bf16[2,16,256]{2,1,0:T(8,128)(2,1)S(1)}, bf16[2,16,256]{2,1,0:T(8,128)(2,1)S(1)}, u32[]{:S(2)}, u32[]{:S(2)}) collective-permute-start(bf16[2,16,256]{2,1,0:T(8,128)(2,1)S(1)} %pad_maximum_fusion.1), channel_id=1, source_target_pairs={{0,7},{1,6},{2,5},{3,4},{4,3},{5,2},{6,1},{7,0},{8,15},{9,14},{10,... | collective-permute-start | bytes 49160 | tf_op jit(solution)/shard_map/ppermute | solution.py:100
  11.5 0.1 collective-permute-start.2
  11.6 0.0 collective-permute-done.1
  11.6 3.1 %collective-permute-done.2 = bf16[2,16,256]{2,1,0:T(8,128)(2,1)S(1)} collective-permute-done((bf16[2,16,256]{2,1,0:T(8,128)(2,1)S(1)}, bf16[2,16,256]{2,1,0:T(8,128)(2,1)S(1)}, u32[]{:S(2)}, u32[]{:S(2)}) %collective-permute-start.2) | collective-permute-done | bytes 16416 | tf_op jit(solution)/shard_map/ppermute | solution.py:100
  14.6 0.0 collective-permute-done.3
  14.7 0.2 %collective-permute-start.4 = (bf16[8,16,256]{2,1,0:T(8,128)(2,1)S(1)}, bf16[8,16,256]{2,1,0:T(8,128)(2,1)S(1)}, u32[]{:S(2)}, u32[]{:S(2)}) collective-permute-start(bf16[8,16,256]{2,1,0:T(8,128)(2,1)S(1)} %constant_dynamic-update-slice_fusion.had_ref), channel_id=1, source_target_pairs={{0,1},{1,0},{2,3},{3,2},{4,5},{5,4},{6,7},{7,6},{8,9},{9,8},{10,11... | collective-permute-start | bytes 196616 | tf_op jit(solution)/shard_map/ppermute | solution.py:100
  14.9 1.1 %collective-permute-done.4.got_ref = bf16[8,16,256]{2,1,0:T(8,128)(2,1)S(1)} collective-permute-done((bf16[8,16,256]{2,1,0:T(8,128)(2,1)S(1)}, bf16[8,16,256]{2,1,0:T(8,128)(2,1)S(1)}, u32[]{:S(2)}, u32[]{:S(2)}) %collective-permute-start.4) | collective-permute-done | bytes 65568 | tf_op jit(solution)/shard_map/ppermute | solution.py:100
  16.0 1.4 %powers.1 = f32[2048,128]{1,0:T(8,128)} custom-call(bf16[8,16,256]{2,1,0:T(8,128)(2,1)S(1)} %constant_dynamic-update-slice_fusion.had_ref, bf16[8,16,256]{2,1,0:T(8,128)(2,1)S(1)} %collective-permute-done.4.got_ref), custom_call_target="tpu_custom_call" | custom-call | tf_op jit(solution)/shard_map/powers/pallas_call | solution.py:184
  (12 shorter events, 0.0 us)
Async XLA Ops:
  3.1 5.0 %collective-permute-start = (bf16[2,16,256]{2,1,0:T(8,128)(2,1)S(1)}, bf16[2,16,256]{2,1,0:T(8,128)(2,1)S(1)}, u32[]{:S(2)}, u32[]{:S(2)}) collective-permute-start(bf16[2,16,256]{2,1,0:T(8,128)(2,1)S(1)} %slice.52), channel_id=1, source_target_pairs={{0,9},{1,8},{2,11},{3,10},{4,13},{5,12},{6,15},{7,14},{8,1},{9,0},... | collective-permute-start | bytes 49160 | tf_op jit(solution)/shard_map/ppermute | solution.py:100
  8.1 3.5 %collective-permute-start.1 = (bf16[2,16,256]{2,1,0:T(8,128)(2,1)S(1)}, bf16[2,16,256]{2,1,0:T(8,128)(2,1)S(1)}, u32[]{:S(2)}, u32[]{:S(2)}) collective-permute-start(bf16[2,16,256]{2,1,0:T(8,128)(2,1)S(1)} %pad_maximum_fusion), channel_id=1, source_target_pairs={{0,3},{1,2},{2,1},{3,0},{4,7},{5,6},{6,5},{7,4},{8,11},{9,10},{10,... | collective-permute-start | bytes 49160 | tf_op jit(solution)/shard_map/ppermute | solution.py:100
  9.9 4.8 %collective-permute-start.3 = (bf16[2,16,256]{2,1,0:T(8,128)(2,1)S(1)}, bf16[2,16,256]{2,1,0:T(8,128)(2,1)S(1)}, u32[]{:S(2)}, u32[]{:S(2)}) collective-permute-start(bf16[2,16,256]{2,1,0:T(8,128)(2,1)S(1)} %pad_maximum_fusion.1), channel_id=1, source_target_pairs={{0,7},{1,6},{2,5},{3,4},{4,3},{5,2},{6,1},{7,0},{8,15},{9,14},{10,... | collective-permute-start | bytes 49160 | tf_op jit(solution)/shard_map/ppermute | solution.py:100
  11.5 3.2 %collective-permute-start.2 = (bf16[2,16,256]{2,1,0:T(8,128)(2,1)S(1)}, bf16[2,16,256]{2,1,0:T(8,128)(2,1)S(1)}, u32[]{:S(2)}, u32[]{:S(2)}) collective-permute-start(bf16[2,16,256]{2,1,0:T(8,128)(2,1)S(1)} %pad_maximum_fusion.1), channel_id=1, source_target_pairs={{0,5},{1,4},{2,7},{3,6},{4,1},{5,0},{6,3},{7,2},{8,13},{9,12},{10,... | collective-permute-start | bytes 49160 | tf_op jit(solution)/shard_map/ppermute | solution.py:100
  14.7 1.3 %collective-permute-start.4 = (bf16[8,16,256]{2,1,0:T(8,128)(2,1)S(1)}, bf16[8,16,256]{2,1,0:T(8,128)(2,1)S(1)}, u32[]{:S(2)}, u32[]{:S(2)}) collective-permute-start(bf16[8,16,256]{2,1,0:T(8,128)(2,1)S(1)} %constant_dynamic-update-slice_fusion.had_ref), channel_id=1, source_target_pairs={{0,1},{1,0},{2,3},{3,2},{4,5},{5,4},{6,7},{7,6},{8,9},{9,8},{10,11... | collective-permute-start | bytes 196616 | tf_op jit(solution)/shard_map/ppermute | solution.py:100

commit v4 on v3

--- a/solution.py
+++ b/solution.py
@@ -13,16 +13,27 @@
 CH_DEV = 2
 PARTS = 2
 LANES = 128
+CHUNK = 1024
+WRITES = 4
 AXES = ("chan", "tgrp", "pol")
 
 
-def twiddle_table(length, blocks):
-    channel = BAND_START + np.arange(blocks * CH_DEV, dtype=np.int64)
-    phase = (channel[:, None] * np.arange(length, dtype=np.int64)) % length
+def turn_of(samples, channels, length):
+    phase = (channels[:, None] * samples) % length
     angles = phase * (2.0 * math.pi / length)
-    table = np.stack([np.cos(angles), -np.sin(angles)], 0)
-    table = table.reshape(PARTS, blocks, CH_DEV, length).transpose(1, 0, 2, 3)
-    return table.reshape(blocks * PARTS * CH_DEV, length).astype(np.float32)
+    both = np.stack([np.cos(angles), -np.sin(angles)], 0)
+    return both.reshape(PARTS, -1, CH_DEV, samples.size).transpose(1, 0, 2, 3)
+
+
+def twiddle_tables(length, blocks, chunk):
+    channels = BAND_START + np.arange(blocks * CH_DEV, dtype=np.int64)
+    first = turn_of(np.arange(chunk, dtype=np.int64), channels, length)
+    crossed = np.stack([-first[:, 1], first[:, 0]], 1)
+    starts = turn_of(np.arange(0, length, chunk, dtype=np.int64), channels, length)
+    steps = np.concatenate([np.stack([starts[:, part]] * PARTS, 1) for part in range(PARTS)], -1)
+    steps = steps.reshape(-1, steps.shape[-1])
+    steps = np.pad(steps, ((0, 0), (0, -steps.shape[1] % LANES)))
+    return np.concatenate([x.reshape(steps.shape[0], -1) for x in (first, crossed, steps)], 1).astype(np.float32)
 
 
 def transform_kernel(chunk, voltages_hbm, taps_hbm, twiddle_hbm, out_ref, volts, taps_ref, table, weights, sems):
@@ -32,10 +43,10 @@
     rows = table.shape[0]
     per_block = PARTS * CH_DEV
     blocks = rows // per_block
-    taps_copy = pltpu.make_async_copy(taps_hbm, taps_ref, sems.at[0])
-    table_copy = pltpu.make_async_copy(twiddle_hbm, table, sems.at[1])
+    table_copy = pltpu.make_async_copy(twiddle_hbm, table, sems.at[0])
+    taps_copy = pltpu.make_async_copy(taps_hbm, taps_ref, sems.at[1])
+    table_copy.start()
     taps_copy.start()
-    table_copy.start()
     volts_copies = [
         pltpu.make_async_copy(
             voltages_hbm.at[pl.ds(step * chunk, chunk)], volts.at[pl.ds(step * chunk, chunk)], sems.at[2 + step]
@@ -44,11 +55,16 @@
     ]
     for copy in volts_copies:
         copy.start()
+    table_copy.wait()
     taps_copy.wait()
-    table_copy.wait()
+    first, crossed = table[:, :chunk], table[:, chunk:2 * chunk]
     for step in range(chunks):
         part = pl.ds(step * chunk, chunk)
-        turns = table[:, part]
+        turns = first
+        if step:
+            turns = first * table[:, 2 * chunk + step:2 * chunk + step + 1]
+            step_sin = 2 * chunk + chunks + step
+            turns = turns + crossed * table[:, step_sin:step_sin + 1]
         for t in range(taps):
             exact = turns * taps_ref[t:t + 1, part]
             high = exact.astype(jnp.bfloat16)
@@ -70,22 +86,24 @@
         out_ref[lax.bitwise_xor(mine, block)] = jnp.concatenate(pieces, 0).astype(out_ref.dtype)
 
 
-def transform(voltages, filter_taps, twiddle):
+def transform(voltages, filter_taps):
     length, inputs = voltages.shape
     taps = filter_taps.shape[0]
-    rows = twiddle.shape[0]
-    chunk = min(length, 1024)
+    chunk = min(length, CHUNK)
     chunks = length // chunk
+    blocks = lax.axis_size("chan")
+    twiddle = jnp.asarray(twiddle_tables(length, blocks, chunk))
     per_block = PARTS * CH_DEV
+    rows = blocks * per_block
     return pl.pallas_call(
         functools.partial(transform_kernel, chunk),
-        out_shape=jax.ShapeDtypeStruct((rows // per_block, taps * per_block, inputs), jnp.bfloat16),
+        out_shape=jax.ShapeDtypeStruct((blocks, taps * per_block, inputs), jnp.bfloat16),
         in_specs=[pl.BlockSpec(memory_space=pltpu.HBM)] * 3,
         out_specs=pl.BlockSpec(memory_space=pltpu.VMEM),
         scratch_shapes=[
             pltpu.VMEM((length, inputs), jnp.bfloat16),
             pltpu.VMEM((taps, length), jnp.float32),
-            pltpu.VMEM((rows, length), jnp.float32),
+            pltpu.VMEM(twiddle.shape, jnp.float32),
             pltpu.VMEM((2 * taps * rows, length), jnp.bfloat16),
             pltpu.SemaphoreType.DMA((2 + chunks,)),
         ],
@@ -126,7 +144,7 @@
     return jnp.concatenate([held[frame][0] for frame in order], 0), [held[frame][1] for frame in order]
 
 
-def power_kernel(taps, groups, scale, halves, had_ref, got_ref, out_ref, terms):
+def power_kernel(taps, groups, scale, halves, had_ref, got_ref, out_hbm, terms, made, sems):
     frames, columns = terms.shape[1], terms.shape[3]
     per_tap = PARTS * CH_DEV
     tiles = columns // LANES
@@ -168,12 +186,25 @@
         ],
         1,
     ).astype(jnp.bfloat16)
-    product = scale * lax.dot_general(
-        left.astype(jnp.bfloat16), against, (((0,), (0,)), ((), ())), preferred_element_type=jnp.float32
-    )
+    left = left.astype(jnp.bfloat16)
     per_row = CH_DEV * tiles * PARTS
-    for index in range(per_row):
-        out_ref[pl.ds(index, rows, stride=per_row), :] = product[:, index * LANES:(index + 1) * LANES]
+    part_rows = max(rows // WRITES, 8)
+    copies = []
+    for step in range(rows // part_rows):
+        product = scale * lax.dot_general(
+            left[:, step * part_rows:(step + 1) * part_rows],
+            against,
+            (((0,), (0,)), ((), ())),
+            preferred_element_type=jnp.float32,
+        )
+        start = step * part_rows * per_row
+        for index in range(per_row):
+            made[pl.ds(start + index, part_rows, stride=per_row), :] = product[:, index * LANES:(index + 1) * LANES]
+        span = pl.ds(start, part_rows * per_row)
+        copies.append(pltpu.make_async_copy(made.at[span], out_hbm.at[span], sems.at[step]))
+        copies[-1].start()
+    for copy in copies:
+        copy.wait()
 
 
 def powers(had, halves, taps):
@@ -185,8 +216,12 @@
         functools.partial(power_kernel, taps, groups, 1.0 / frames, halves),
         out_shape=jax.ShapeDtypeStruct((rows * CH_DEV * tiles * PARTS, LANES), jnp.float32),
         in_specs=[pl.BlockSpec(memory_space=pltpu.VMEM)] * 2,
-        out_specs=pl.BlockSpec(memory_space=pltpu.VMEM),
-        scratch_shapes=[pltpu.VMEM((2, frames, depth, columns), jnp.bfloat16)],
+        out_specs=pl.BlockSpec(memory_space=pltpu.HBM),
+        scratch_shapes=[
+            pltpu.VMEM((2, frames, depth, columns), jnp.bfloat16),
+            pltpu.VMEM((rows * CH_DEV * tiles * PARTS, LANES), jnp.float32),
+            pltpu.SemaphoreType.DMA((WRITES,)),
+        ],
         compiler_params=pltpu.CompilerParams(vmem_limit_bytes=32 * 2**20),
         name="powers",
     )(had, moved(had, 0, 1))
@@ -195,8 +230,7 @@
 
 
 def body(voltages, filter_taps):
-    twiddle = jnp.asarray(twiddle_table(voltages.shape[1], lax.axis_size("chan")))
-    terms = transform(voltages[0], filter_taps, twiddle)
+    terms = transform(voltages[0], filter_taps)
     had, halves = exchanged(terms)
     return powers(had, halves, filter_taps.shape[0])
 

time: 17.5 us -> 17.4 us (level)
  no operation moved by 1% of the time
where the time goes in v4:
time: 17.4 us; the launch traced here: 17.2 us
  starting transfers between devices  7.19 us (41%)
  waiting for transfers between devices  5.66 us (33%)
  Pallas kernels  4.27 us (25%)
    ppermute x5, starting transfers between devices, moved(): lax.ppermute(array, AXES, [(i, i ^ frame_bits * 2 + swap) for i in range(...  7.19 us
    ppermute x5, waiting for transfers between devices, moved(): lax.ppermute(array, AXES, [(i, i ^ frame_bits * 2 + swap) for i in range(...  5.66 us
    pallas_call x1, Pallas kernels, transform(): pl.pallas_call(functools.partial(transform_kernel, chunk), out_shape=jax....  3 us
    pallas_call x1, Pallas kernels, powers(): pl.pallas_call(functools.partial(power_kernel, taps, groups, 1.0 / frames...  1.27 us
  transfers between devices with their start and end apart: 5, of which 3 were waited for; matrix products, arithmetic and copies ran while one was open for 0% of the time, Pallas kernels for 0%

profile of v4, /device:TPU:0, one launch (start us, length us, event | category | flops | bytes accessed | tf_op | source)
XLA Modules:
  0.0 17.2 jit_solution(2936370449507526875)
XLA Ops:
  0.0 3.0 %transform.1 = bf16[4,16,256]{2,1,0:T(8,128)(2,1)S(1)} custom-call(bf16[8192,256]{1,0:T(8,128)(2,1)} %bitcast.6, f32[4,8192]{1,0:T(4,128)} %taps_hbm.1, f32[16,2176]{1,0:T(8,128)} %constant.2.clone.twiddle_hbm), custom_call_target="tpu_custom_call" | custom-call | tf_op jit(solution)/shard_map/transform/pallas_call | solution.py:98
  3.0 3.5 %collective-permute-start = (bf16[2,16,256]{2,1,0:T(8,128)(2,1)S(1)}, bf16[2,16,256]{2,1,0:T(8,128)(2,1)S(1)}, u32[]{:S(2)}, u32[]{:S(2)}) collective-permute-start(bf16[2,16,256]{2,1,0:T(8,128)(2,1)S(1)} %slice.52), channel_id=1, source_target_pairs={{0,9},{1,8},{2,11},{3,10},{4,13},{5,12},{6,15},{7,14},{8,1},{9,0},... | collective-permute-start | bytes 49160 | tf_op jit(solution)/shard_map/ppermute | solution.py:118
  6.6 1.4 %collective-permute-done = bf16[2,16,256]{2,1,0:T(8,128)(2,1)S(1)} collective-permute-done((bf16[2,16,256]{2,1,0:T(8,128)(2,1)S(1)}, bf16[2,16,256]{2,1,0:T(8,128)(2,1)S(1)}, u32[]{:S(2)}, u32[]{:S(2)}) %collective-permute-start) | collective-permute-done | bytes 16416 | tf_op jit(solution)/shard_map/ppermute | solution.py:118
  8.0 1.8 %collective-permute-start.1 = (bf16[2,16,256]{2,1,0:T(8,128)(2,1)S(1)}, bf16[2,16,256]{2,1,0:T(8,128)(2,1)S(1)}, u32[]{:S(2)}, u32[]{:S(2)}) collective-permute-start(bf16[2,16,256]{2,1,0:T(8,128)(2,1)S(1)} %pad_maximum_fusion), channel_id=1, source_target_pairs={{0,3},{1,2},{2,1},{3,0},{4,7},{5,6},{6,5},{7,4},{8,11},{9,10},{10,... | collective-permute-start | bytes 49160 | tf_op jit(solution)/shard_map/ppermute | solution.py:118
  9.8 1.6 %collective-permute-start.3 = (bf16[2,16,256]{2,1,0:T(8,128)(2,1)S(1)}, bf16[2,16,256]{2,1,0:T(8,128)(2,1)S(1)}, u32[]{:S(2)}, u32[]{:S(2)}) collective-permute-start(bf16[2,16,256]{2,1,0:T(8,128)(2,1)S(1)} %pad_maximum_fusion.1), channel_id=1, source_target_pairs={{0,7},{1,6},{2,5},{3,4},{4,3},{5,2},{6,1},{7,0},{8,15},{9,14},{10,... | collective-permute-start | bytes 49160 | tf_op jit(solution)/shard_map/ppermute | solution.py:118
  11.4 0.1 collective-permute-start.2
  11.5 0.0 collective-permute-done.1
  11.5 3.1 %collective-permute-done.2 = bf16[2,16,256]{2,1,0:T(8,128)(2,1)S(1)} collective-permute-done((bf16[2,16,256]{2,1,0:T(8,128)(2,1)S(1)}, bf16[2,16,256]{2,1,0:T(8,128)(2,1)S(1)}, u32[]{:S(2)}, u32[]{:S(2)}) %collective-permute-start.2) | collective-permute-done | bytes 16416 | tf_op jit(solution)/shard_map/ppermute | solution.py:118
  14.6 0.0 collective-permute-done.3
  14.6 0.2 %collective-permute-start.4 = (bf16[8,16,256]{2,1,0:T(8,128)(2,1)S(1)}, bf16[8,16,256]{2,1,0:T(8,128)(2,1)S(1)}, u32[]{:S(2)}, u32[]{:S(2)}) collective-permute-start(bf16[8,16,256]{2,1,0:T(8,128)(2,1)S(1)} %constant_dynamic-update-slice_fusion.had_ref), channel_id=1, source_target_pairs={{0,1},{1,0},{2,3},{3,2},{4,5},{5,4},{6,7},{7,6},{8,9},{9,8},{10,11... | collective-permute-start | bytes 196616 | tf_op jit(solution)/shard_map/ppermute | solution.py:118
  14.8 1.1 %collective-permute-done.4.got_ref = bf16[8,16,256]{2,1,0:T(8,128)(2,1)S(1)} collective-permute-done((bf16[8,16,256]{2,1,0:T(8,128)(2,1)S(1)}, bf16[8,16,256]{2,1,0:T(8,128)(2,1)S(1)}, u32[]{:S(2)}, u32[]{:S(2)}) %collective-permute-start.4) | collective-permute-done | bytes 65568 | tf_op jit(solution)/shard_map/ppermute | solution.py:118
  15.9 1.3 %powers.1 = f32[2048,128]{1,0:T(8,128)} custom-call(bf16[8,16,256]{2,1,0:T(8,128)(2,1)S(1)} %constant_dynamic-update-slice_fusion.had_ref, bf16[8,16,256]{2,1,0:T(8,128)(2,1)S(1)} %collective-permute-done.4.got_ref), custom_call_target="tpu_custom_call" | custom-call | tf_op jit(solution)/shard_map/powers/pallas_call | solution.py:215
  (12 shorter events, 0.0 us)
Async XLA Ops:
  3.0 5.0 %collective-permute-start = (bf16[2,16,256]{2,1,0:T(8,128)(2,1)S(1)}, bf16[2,16,256]{2,1,0:T(8,128)(2,1)S(1)}, u32[]{:S(2)}, u32[]{:S(2)}) collective-permute-start(bf16[2,16,256]{2,1,0:T(8,128)(2,1)S(1)} %slice.52), channel_id=1, source_target_pairs={{0,9},{1,8},{2,11},{3,10},{4,13},{5,12},{6,15},{7,14},{8,1},{9,0},... | collective-permute-start | bytes 49160 | tf_op jit(solution)/shard_map/ppermute | solution.py:118
  8.0 3.5 %collective-permute-start.1 = (bf16[2,16,256]{2,1,0:T(8,128)(2,1)S(1)}, bf16[2,16,256]{2,1,0:T(8,128)(2,1)S(1)}, u32[]{:S(2)}, u32[]{:S(2)}) collective-permute-start(bf16[2,16,256]{2,1,0:T(8,128)(2,1)S(1)} %pad_maximum_fusion), channel_id=1, source_target_pairs={{0,3},{1,2},{2,1},{3,0},{4,7},{5,6},{6,5},{7,4},{8,11},{9,10},{10,... | collective-permute-start | bytes 49160 | tf_op jit(solution)/shard_map/ppermute | solution.py:118
  9.8 4.8 %collective-permute-start.3 = (bf16[2,16,256]{2,1,0:T(8,128)(2,1)S(1)}, bf16[2,16,256]{2,1,0:T(8,128)(2,1)S(1)}, u32[]{:S(2)}, u32[]{:S(2)}) collective-permute-start(bf16[2,16,256]{2,1,0:T(8,128)(2,1)S(1)} %pad_maximum_fusion.1), channel_id=1, source_target_pairs={{0,7},{1,6},{2,5},{3,4},{4,3},{5,2},{6,1},{7,0},{8,15},{9,14},{10,... | collective-permute-start | bytes 49160 | tf_op jit(solution)/shard_map/ppermute | solution.py:118
  11.4 3.2 %collective-permute-start.2 = (bf16[2,16,256]{2,1,0:T(8,128)(2,1)S(1)}, bf16[2,16,256]{2,1,0:T(8,128)(2,1)S(1)}, u32[]{:S(2)}, u32[]{:S(2)}) collective-permute-start(bf16[2,16,256]{2,1,0:T(8,128)(2,1)S(1)} %pad_maximum_fusion.1), channel_id=1, source_target_pairs={{0,5},{1,4},{2,7},{3,6},{4,1},{5,0},{6,3},{7,2},{8,13},{9,12},{10,... | collective-permute-start | bytes 49160 | tf_op jit(solution)/shard_map/ppermute | solution.py:118
  14.6 1.3 %collective-permute-start.4 = (bf16[8,16,256]{2,1,0:T(8,128)(2,1)S(1)}, bf16[8,16,256]{2,1,0:T(8,128)(2,1)S(1)}, u32[]{:S(2)}, u32[]{:S(2)}) collective-permute-start(bf16[8,16,256]{2,1,0:T(8,128)(2,1)S(1)} %constant_dynamic-update-slice_fusion.had_ref), channel_id=1, source_target_pairs={{0,1},{1,0},{2,3},{3,2},{4,5},{5,4},{6,7},{7,6},{8,9},{9,8},{10,11... | collective-permute-start | bytes 196616 | tf_op jit(solution)/shard_map/ppermute | solution.py:118

commit v5 on v4

--- a/solution.py
+++ b/solution.py
@@ -14,6 +14,7 @@
 PARTS = 2
 LANES = 128
 CHUNK = 1024
+ENDS = (1, 3, 6, 8)
 WRITES = 4
 AXES = ("chan", "tgrp", "pol")
 
@@ -73,10 +74,16 @@
                 exact - high.astype(jnp.float32)
             ).astype(jnp.bfloat16)
     total = jnp.zeros((2 * taps * rows, volts.shape[1]), jnp.float32)
-    for step in range(chunks):
-        part = pl.ds(step * chunk, chunk)
-        volts_copies[step].wait()
+    start = 0
+    for eighths in ENDS:
+        stop = chunks * eighths // 8
+        if stop == start:
+            continue
+        for copy in volts_copies[start:stop]:
+            copy.wait()
+        part = pl.ds(start * chunk, (stop - start) * chunk)
         total = total + jnp.dot(weights[:, part], volts[part], preferred_element_type=jnp.float32)
+        start = stop
     total = total[:taps * rows] + total[taps * rows:]
     mine = lax.axis_index("chan")
     for block in range(blocks):
@@ -219,7 +226,7 @@
         out_specs=pl.BlockSpec(memory_space=pltpu.HBM),
         scratch_shapes=[
             pltpu.VMEM((2, frames, depth, columns), jnp.bfloat16),
-            pltpu.VMEM((rows * CH_DEV * tiles * PARTS, LANES), jnp.float32),
+            pltpu.VMEM(((rows + 1) * CH_DEV * tiles * PARTS, LANES), jnp.float32),
             pltpu.SemaphoreType.DMA((WRITES,)),
         ],
         compiler_params=pltpu.CompilerParams(vmem_limit_bytes=32 * 2**20),

time: 17.4 us -> 17.2 us (0.989)
  Pallas kernels: 4.27 us -> 4.09 us
    pallas_call x1, Pallas kernels: 3 us -> 2.81 us  [transform(): pl.pallas_call(functools.partial(transform_kernel, chunk), out_shape=jax....]
where the time goes in v5:
time: 17.2 us; the launch traced here: 17 us
  starting transfers between devices  7.19 us (42%)
  waiting for transfers between devices  5.66 us (33%)
  Pallas kernels  4.09 us (24%)
    ppermute x5, starting transfers between devices, moved(): lax.ppermute(array, AXES, [(i, i ^ frame_bits * 2 + swap) for i in range(...  7.19 us
    ppermute x5, waiting for transfers between devices, moved(): lax.ppermute(array, AXES, [(i, i ^ frame_bits * 2 + swap) for i in range(...  5.66 us
    pallas_call x1, Pallas kernels, transform(): pl.pallas_call(functools.partial(transform_kernel, chunk), out_shape=jax....  2.81 us
    pallas_call x1, Pallas kernels, powers(): pl.pallas_call(functools.partial(power_kernel, taps, groups, 1.0 / frames...  1.27 us
  transfers between devices with their start and end apart: 5, of which 3 were waited for; matrix products, arithmetic and copies ran while one was open for 0% of the time, Pallas kernels for 0%

profile of v5, /device:TPU:0, one launch (start us, length us, event | category | flops | bytes accessed | tf_op | source)
XLA Modules:
  0.0 17.0 jit_solution(18310601406554056058)
XLA Ops:
  0.0 2.8 %transform.1 = bf16[4,16,256]{2,1,0:T(8,128)(2,1)S(1)} custom-call(bf16[8192,256]{1,0:T(8,128)(2,1)} %bitcast.6, f32[4,8192]{1,0:T(4,128)} %taps_hbm.1, f32[16,2176]{1,0:T(8,128)} %constant.2.clone.twiddle_hbm), custom_call_target="tpu_custom_call" | custom-call | tf_op jit(solution)/shard_map/transform/pallas_call | solution.py:105
  2.8 3.5 %collective-permute-start = (bf16[2,16,256]{2,1,0:T(8,128)(2,1)S(1)}, bf16[2,16,256]{2,1,0:T(8,128)(2,1)S(1)}, u32[]{:S(2)}, u32[]{:S(2)}) collective-permute-start(bf16[2,16,256]{2,1,0:T(8,128)(2,1)S(1)} %slice.52), channel_id=1, source_target_pairs={{0,9},{1,8},{2,11},{3,10},{4,13},{5,12},{6,15},{7,14},{8,1},{9,0},... | collective-permute-start | bytes 49160 | tf_op jit(solution)/shard_map/ppermute | solution.py:125
  6.4 1.4 %collective-permute-done = bf16[2,16,256]{2,1,0:T(8,128)(2,1)S(1)} collective-permute-done((bf16[2,16,256]{2,1,0:T(8,128)(2,1)S(1)}, bf16[2,16,256]{2,1,0:T(8,128)(2,1)S(1)}, u32[]{:S(2)}, u32[]{:S(2)}) %collective-permute-start) | collective-permute-done | bytes 16416 | tf_op jit(solution)/shard_map/ppermute | solution.py:125
  7.8 1.8 %collective-permute-start.1 = (bf16[2,16,256]{2,1,0:T(8,128)(2,1)S(1)}, bf16[2,16,256]{2,1,0:T(8,128)(2,1)S(1)}, u32[]{:S(2)}, u32[]{:S(2)}) collective-permute-start(bf16[2,16,256]{2,1,0:T(8,128)(2,1)S(1)} %pad_maximum_fusion), channel_id=1, source_target_pairs={{0,3},{1,2},{2,1},{3,0},{4,7},{5,6},{6,5},{7,4},{8,11},{9,10},{10,... | collective-permute-start | bytes 49160 | tf_op jit(solution)/shard_map/ppermute | solution.py:125
  9.6 1.6 %collective-permute-start.3 = (bf16[2,16,256]{2,1,0:T(8,128)(2,1)S(1)}, bf16[2,16,256]{2,1,0:T(8,128)(2,1)S(1)}, u32[]{:S(2)}, u32[]{:S(2)}) collective-permute-start(bf16[2,16,256]{2,1,0:T(8,128)(2,1)S(1)} %pad_maximum_fusion.1), channel_id=1, source_target_pairs={{0,7},{1,6},{2,5},{3,4},{4,3},{5,2},{6,1},{7,0},{8,15},{9,14},{10,... | collective-permute-start | bytes 49160 | tf_op jit(solution)/shard_map/ppermute | solution.py:125
  11.2 0.1 collective-permute-start.2
  11.3 0.0 collective-permute-done.1
  11.3 3.1 %collective-permute-done.2 = bf16[2,16,256]{2,1,0:T(8,128)(2,1)S(1)} collective-permute-done((bf16[2,16,256]{2,1,0:T(8,128)(2,1)S(1)}, bf16[2,16,256]{2,1,0:T(8,128)(2,1)S(1)}, u32[]{:S(2)}, u32[]{:S(2)}) %collective-permute-start.2) | collective-permute-done | bytes 16416 | tf_op jit(solution)/shard_map/ppermute | solution.py:125
  14.4 0.0 collective-permute-done.3
  14.4 0.2 %collective-permute-start.4 = (bf16[8,16,256]{2,1,0:T(8,128)(2,1)S(1)}, bf16[8,16,256]{2,1,0:T(8,128)(2,1)S(1)}, u32[]{:S(2)}, u32[]{:S(2)}) collective-permute-start(bf16[8,16,256]{2,1,0:T(8,128)(2,1)S(1)} %constant_dynamic-update-slice_fusion.had_ref), channel_id=1, source_target_pairs={{0,1},{1,0},{2,3},{3,2},{4,5},{5,4},{6,7},{7,6},{8,9},{9,8},{10,11... | collective-permute-start | bytes 196616 | tf_op jit(solution)/shard_map/ppermute | solution.py:125
  14.6 1.1 %collective-permute-done.4.got_ref = bf16[8,16,256]{2,1,0:T(8,128)(2,1)S(1)} collective-permute-done((bf16[8,16,256]{2,1,0:T(8,128)(2,1)S(1)}, bf16[8,16,256]{2,1,0:T(8,128)(2,1)S(1)}, u32[]{:S(2)}, u32[]{:S(2)}) %collective-permute-start.4) | collective-permute-done | bytes 65568 | tf_op jit(solution)/shard_map/ppermute | solution.py:125
  15.7 1.3 %powers.1 = f32[2048,128]{1,0:T(8,128)} custom-call(bf16[8,16,256]{2,1,0:T(8,128)(2,1)S(1)} %constant_dynamic-update-slice_fusion.had_ref, bf16[8,16,256]{2,1,0:T(8,128)(2,1)S(1)} %collective-permute-done.4.got_ref), custom_call_target="tpu_custom_call" | custom-call | tf_op jit(solution)/shard_map/powers/pallas_call | solution.py:222
  (12 shorter events, 0.0 us)
Async XLA Ops:
  2.8 5.0 %collective-permute-start = (bf16[2,16,256]{2,1,0:T(8,128)(2,1)S(1)}, bf16[2,16,256]{2,1,0:T(8,128)(2,1)S(1)}, u32[]{:S(2)}, u32[]{:S(2)}) collective-permute-start(bf16[2,16,256]{2,1,0:T(8,128)(2,1)S(1)} %slice.52), channel_id=1, source_target_pairs={{0,9},{1,8},{2,11},{3,10},{4,13},{5,12},{6,15},{7,14},{8,1},{9,0},... | collective-permute-start | bytes 49160 | tf_op jit(solution)/shard_map/ppermute | solution.py:125
  7.8 3.5 %collective-permute-start.1 = (bf16[2,16,256]{2,1,0:T(8,128)(2,1)S(1)}, bf16[2,16,256]{2,1,0:T(8,128)(2,1)S(1)}, u32[]{:S(2)}, u32[]{:S(2)}) collective-permute-start(bf16[2,16,256]{2,1,0:T(8,128)(2,1)S(1)} %pad_maximum_fusion), channel_id=1, source_target_pairs={{0,3},{1,2},{2,1},{3,0},{4,7},{5,6},{6,5},{7,4},{8,11},{9,10},{10,... | collective-permute-start | bytes 49160 | tf_op jit(solution)/shard_map/ppermute | solution.py:125
  9.6 4.8 %collective-permute-start.3 = (bf16[2,16,256]{2,1,0:T(8,128)(2,1)S(1)}, bf16[2,16,256]{2,1,0:T(8,128)(2,1)S(1)}, u32[]{:S(2)}, u32[]{:S(2)}) collective-permute-start(bf16[2,16,256]{2,1,0:T(8,128)(2,1)S(1)} %pad_maximum_fusion.1), channel_id=1, source_target_pairs={{0,7},{1,6},{2,5},{3,4},{4,3},{5,2},{6,1},{7,0},{8,15},{9,14},{10,... | collective-permute-start | bytes 49160 | tf_op jit(solution)/shard_map/ppermute | solution.py:125
  11.2 3.2 %collective-permute-start.2 = (bf16[2,16,256]{2,1,0:T(8,128)(2,1)S(1)}, bf16[2,16,256]{2,1,0:T(8,128)(2,1)S(1)}, u32[]{:S(2)}, u32[]{:S(2)}) collective-permute-start(bf16[2,16,256]{2,1,0:T(8,128)(2,1)S(1)} %pad_maximum_fusion.1), channel_id=1, source_target_pairs={{0,5},{1,4},{2,7},{3,6},{4,1},{5,0},{6,3},{7,2},{8,13},{9,12},{10,... | collective-permute-start | bytes 49160 | tf_op jit(solution)/shard_map/ppermute | solution.py:125
  14.4 1.3 %collective-permute-start.4 = (bf16[8,16,256]{2,1,0:T(8,128)(2,1)S(1)}, bf16[8,16,256]{2,1,0:T(8,128)(2,1)S(1)}, u32[]{:S(2)}, u32[]{:S(2)}) collective-permute-start(bf16[8,16,256]{2,1,0:T(8,128)(2,1)S(1)} %constant_dynamic-update-slice_fusion.had_ref), channel_id=1, source_target_pairs={{0,1},{1,0},{2,3},{3,2},{4,5},{5,4},{6,7},{7,6},{8,9},{9,8},{10,11... | collective-permute-start | bytes 196616 | tf_op jit(solution)/shard_map/ppermute | solution.py:125

commit v6 on v5

--- a/solution.py
+++ b/solution.py
@@ -119,10 +119,16 @@
     )(voltages, filter_taps, twiddle)
 
 
-def moved(array, frame_bits, swap):
-    chans, groups = lax.axis_size("chan"), lax.axis_size("tgrp")
-    count = chans * groups * 2
-    return lax.ppermute(array, AXES, [(i, i ^ (frame_bits * 2 + swap)) for i in range(count)])
+def moved(array, masks):
+    devices = lax.axis_size("chan") * lax.axis_size("tgrp") * 2
+    return lax.ppermute(array, AXES, [(i, i ^ (masks[i % 2] * 2 + 1)) for i in range(devices)])
+
+
+def swapped(payloads, one, other):
+    first = lax.axis_index("pol") == 0
+    early = moved(jnp.where(first, payloads[one], payloads[other]), (one, other))
+    late = moved(jnp.where(first, payloads[other], payloads[one]), (other, one))
+    return {one: jnp.where(first, late, early), other: jnp.where(first, early, late)}
 
 
 def exchanged(terms):
@@ -139,13 +145,20 @@
             index = sum(1 << i for i, bit in enumerate(reversed(of_chan)) if mask & bit)
             return value[index * count:(index + 1) * count]
 
+        def payload(mask):
+            return jnp.concatenate([blocks_for(value, mask) for value, _ in held.values()], 0)
+
+        got = {}
+        if len(bits) == 2:
+            high, low = bits
+            got = swapped({mask: payload(mask) for mask in bits}, low, high)
+        if bits:
+            got[sum(bits)] = moved(payload(sum(bits)), (sum(bits),) * 2)
         kept = {frame: (blocks_for(value, 0), half) for frame, (value, half) in held.items()}
-        masks = [sum(bit for i, bit in enumerate(bits) if pick >> i & 1) for pick in range(1, 1 << len(bits))]
-        for mask in reversed(masks):
-            got = moved(jnp.concatenate([blocks_for(value, mask) for value, _ in held.values()], 0), mask, 1)
-            count = got.shape[0] // len(held)
+        for mask, value in got.items():
+            count = value.shape[0] // len(held)
             for index, (frame, (_, half)) in enumerate(held.items()):
-                kept[frame ^ mask] = (got[index * count:(index + 1) * count], 1 - half)
+                kept[frame ^ mask] = (value[index * count:(index + 1) * count], 1 - half)
         held = kept
     order = sorted(held)
     return jnp.concatenate([held[frame][0] for frame in order], 0), [held[frame][1] for frame in order]
@@ -231,7 +244,7 @@
         ],
         compiler_params=pltpu.CompilerParams(vmem_limit_bytes=32 * 2**20),
         name="powers",
-    )(had, moved(had, 0, 1))
+    )(had, moved(had, (0, 0)))
     out = out.reshape(rows, CH_DEV, tiles, PARTS, LANES).transpose(0, 1, 3, 2, 4)
     return out.reshape(rows, CH_DEV, PARTS, columns)
 

time: 17.2 us -> 16.8 us (0.977)
  waiting for transfers between devices: 5.66 us -> 3.77 us
  starting transfers between devices: 7.19 us -> 8.75 us
    ppermute x5, waiting for transfers between devices: 5.66 us -> 3.77 us  [moved(): lax.ppermute(array, AXES, [(i, i ^ masks[i % 2] * 2 + 1) for i in range(d...]
    ppermute x5, starting transfers between devices: 7.19 us -> 8.75 us  [moved(): lax.ppermute(array, AXES, [(i, i ^ masks[i % 2] * 2 + 1) for i in range(d...]
  transfers between devices with their start and end apart: 5 -> 5, of which waited for: 3 -> 4; matrix products, arithmetic and copies ran while one was open for 0% -> 0% of each run, Pallas kernels for 0% -> 0%
where the time goes in v6:
time: 16.8 us; the launch traced here: 16.7 us
  starting transfers between devices  8.75 us (52%)
  Pallas kernels  4.08 us (24%)
  waiting for transfers between devices  3.77 us (22%)
    ppermute x5, starting transfers between devices, moved(): lax.ppermute(array, AXES, [(i, i ^ masks[i % 2] * 2 + 1) for i in range(d...  8.75 us
    ppermute x5, waiting for transfers between devices, moved(): lax.ppermute(array, AXES, [(i, i ^ masks[i % 2] * 2 + 1) for i in range(d...  3.77 us
    pallas_call x1, Pallas kernels, transform(): pl.pallas_call(functools.partial(transform_kernel, chunk), out_shape=jax....  2.81 us
    pallas_call x1, Pallas kernels, powers(): pl.pallas_call(functools.partial(power_kernel, taps, groups, 1.0 / frames...  1.27 us
  transfers between devices with their start and end apart: 5, of which 4 were waited for; matrix products, arithmetic and copies ran while one was open for 0% of the time, Pallas kernels for 0%

profile of v6, /device:TPU:0, one launch (start us, length us, event | category | flops | bytes accessed | tf_op | source)
XLA Modules:
  0.0 16.7 jit_solution(15083030161311848803)
XLA Ops:
  0.0 2.8 %transform.1 = bf16[4,16,256]{2,1,0:T(8,128)(2,1)S(1)} custom-call(bf16[8192,256]{1,0:T(8,128)(2,1)} %bitcast.6, f32[4,8192]{1,0:T(4,128)} %taps_hbm.1, f32[16,2176]{1,0:T(8,128)} %constant.8.clone.twiddle_hbm), custom_call_target="tpu_custom_call" | custom-call | tf_op jit(solution)/shard_map/transform/pallas_call | solution.py:105
  2.8 3.5 %collective-permute-start = (bf16[2,16,256]{2,1,0:T(8,128)(2,1)S(1)}, bf16[2,16,256]{2,1,0:T(8,128)(2,1)S(1)}, u32[]{:S(2)}, u32[]{:S(2)}) collective-permute-start(bf16[2,16,256]{2,1,0:T(8,128)(2,1)S(1)} %slice.53), channel_id=1, source_target_pairs={{0,9},{1,8},{2,11},{3,10},{4,13},{5,12},{6,15},{7,14},{8,1},{9,0},... | collective-permute-start | bytes 49160 | tf_op jit(solution)/shard_map/ppermute | solution.py:124
  6.4 1.4 %collective-permute-done = bf16[2,16,256]{2,1,0:T(8,128)(2,1)S(1)} collective-permute-done((bf16[2,16,256]{2,1,0:T(8,128)(2,1)S(1)}, bf16[2,16,256]{2,1,0:T(8,128)(2,1)S(1)}, u32[]{:S(2)}, u32[]{:S(2)}) %collective-permute-start) | collective-permute-done | bytes 16416 | tf_op jit(solution)/shard_map/ppermute | solution.py:124
  7.8 1.9 %collective-permute-start.2 = (bf16[2,16,256]{2,1,0:T(8,128)(2,1)S(1)}, bf16[2,16,256]{2,1,0:T(8,128)(2,1)S(1)}, u32[]{:S(2)}, u32[]{:S(2)}) collective-permute-start(bf16[2,16,256]{2,1,0:T(8,128)(2,1)S(1)} %get-tuple-element.7), channel_id=1, source_target_pairs={{0,3},{1,4},{2,1},{3,6},{4,7},{5,0},{6,5},{7,2},{8,11},{9,12},{10,... | collective-permute-start | bytes 49160 | tf_op jit(solution)/shard_map/ppermute | solution.py:124
  9.7 0.2 collective-permute-start.1
  9.8 2.6 %collective-permute-start.3 = (bf16[2,16,256]{2,1,0:T(8,128)(2,1)S(1)}, bf16[2,16,256]{2,1,0:T(8,128)(2,1)S(1)}, u32[]{:S(2)}, u32[]{:S(2)}) collective-permute-start(bf16[2,16,256]{2,1,0:T(8,128)(2,1)S(1)} %get-tuple-element.12), channel_id=1, source_target_pairs={{0,7},{1,6},{2,5},{3,4},{4,3},{5,2},{6,1},{7,0},{8,15},{9,14},{10,... | collective-permute-start | bytes 49160 | tf_op jit(solution)/shard_map/ppermute | solution.py:124
  12.4 0.0 collective-permute-done.2
  12.4 0.4 %collective-permute-done.1 = bf16[2,16,256]{2,1,0:T(8,128)(2,1)S(1)} collective-permute-done((bf16[2,16,256]{2,1,0:T(8,128)(2,1)S(1)}, bf16[2,16,256]{2,1,0:T(8,128)(2,1)S(1)}, u32[]{:S(2)}, u32[]{:S(2)}) %collective-permute-start.1) | collective-permute-done | bytes 16416 | tf_op jit(solution)/shard_map/ppermute | solution.py:124
  12.9 1.0 %collective-permute-done.3 = bf16[2,16,256]{2,1,0:T(8,128)(2,1)S(1)} collective-permute-done((bf16[2,16,256]{2,1,0:T(8,128)(2,1)S(1)}, bf16[2,16,256]{2,1,0:T(8,128)(2,1)S(1)}, u32[]{:S(2)}, u32[]{:S(2)}) %collective-permute-start.3) | collective-permute-done | bytes 16416 | tf_op jit(solution)/shard_map/ppermute | solution.py:124
  13.9 0.6 %collective-permute-start.4 = (bf16[8,16,256]{2,1,0:T(8,128)(2,1)S(1)}, bf16[8,16,256]{2,1,0:T(8,128)(2,1)S(1)}, u32[]{:S(2)}, u32[]{:S(2)}) collective-permute-start(bf16[8,16,256]{2,1,0:T(8,128)(2,1)S(1)} %constant_dynamic-update-slice_fusion.had_ref), channel_id=1, source_target_pairs={{0,1},{1,0},{2,3},{3,2},{4,5},{5,4},{6,7},{7,6},{8,9},{9,8},{10,11... | collective-permute-start | bytes 196616 | tf_op jit(solution)/shard_map/ppermute | solution.py:124
  14.5 0.9 %collective-permute-done.4.got_ref = bf16[8,16,256]{2,1,0:T(8,128)(2,1)S(1)} collective-permute-done((bf16[8,16,256]{2,1,0:T(8,128)(2,1)S(1)}, bf16[8,16,256]{2,1,0:T(8,128)(2,1)S(1)}, u32[]{:S(2)}, u32[]{:S(2)}) %collective-permute-start.4) | collective-permute-done | bytes 65568 | tf_op jit(solution)/shard_map/ppermute | solution.py:124
  15.4 1.3 %powers.1 = f32[2048,128]{1,0:T(8,128)} custom-call(bf16[8,16,256]{2,1,0:T(8,128)(2,1)S(1)} %constant_dynamic-update-slice_fusion.had_ref, bf16[8,16,256]{2,1,0:T(8,128)(2,1)S(1)} %collective-permute-done.4.got_ref), custom_call_target="tpu_custom_call" | custom-call | tf_op jit(solution)/shard_map/powers/pallas_call | solution.py:235
  (12 shorter events, 0.0 us)
Async XLA Ops:
  2.8 5.0 %collective-permute-start = (bf16[2,16,256]{2,1,0:T(8,128)(2,1)S(1)}, bf16[2,16,256]{2,1,0:T(8,128)(2,1)S(1)}, u32[]{:S(2)}, u32[]{:S(2)}) collective-permute-start(bf16[2,16,256]{2,1,0:T(8,128)(2,1)S(1)} %slice.53), channel_id=1, source_target_pairs={{0,9},{1,8},{2,11},{3,10},{4,13},{5,12},{6,15},{7,14},{8,1},{9,0},... | collective-permute-start | bytes 49160 | tf_op jit(solution)/shard_map/ppermute | solution.py:124
  7.8 4.6 %collective-permute-start.2 = (bf16[2,16,256]{2,1,0:T(8,128)(2,1)S(1)}, bf16[2,16,256]{2,1,0:T(8,128)(2,1)S(1)}, u32[]{:S(2)}, u32[]{:S(2)}) collective-permute-start(bf16[2,16,256]{2,1,0:T(8,128)(2,1)S(1)} %get-tuple-element.7), channel_id=1, source_target_pairs={{0,3},{1,4},{2,1},{3,6},{4,7},{5,0},{6,5},{7,2},{8,11},{9,12},{10,... | collective-permute-start | bytes 49160 | tf_op jit(solution)/shard_map/ppermute | solution.py:124
  9.7 3.2 %collective-permute-start.1 = (bf16[2,16,256]{2,1,0:T(8,128)(2,1)S(1)}, bf16[2,16,256]{2,1,0:T(8,128)(2,1)S(1)}, u32[]{:S(2)}, u32[]{:S(2)}) collective-permute-start(bf16[2,16,256]{2,1,0:T(8,128)(2,1)S(1)} %get-tuple-element.8), channel_id=1, source_target_pairs={{0,5},{1,2},{2,7},{3,0},{4,1},{5,6},{6,3},{7,4},{8,13},{9,10},{10,... | collective-permute-start | bytes 49160 | tf_op jit(solution)/shard_map/ppermute | solution.py:124
  9.8 4.1 %collective-permute-start.3 = (bf16[2,16,256]{2,1,0:T(8,128)(2,1)S(1)}, bf16[2,16,256]{2,1,0:T(8,128)(2,1)S(1)}, u32[]{:S(2)}, u32[]{:S(2)}) collective-permute-start(bf16[2,16,256]{2,1,0:T(8,128)(2,1)S(1)} %get-tuple-element.12), channel_id=1, source_target_pairs={{0,7},{1,6},{2,5},{3,4},{4,3},{5,2},{6,1},{7,0},{8,15},{9,14},{10,... | collective-permute-start | bytes 49160 | tf_op jit(solution)/shard_map/ppermute | solution.py:124
  13.9 1.5 %collective-permute-start.4 = (bf16[8,16,256]{2,1,0:T(8,128)(2,1)S(1)}, bf16[8,16,256]{2,1,0:T(8,128)(2,1)S(1)}, u32[]{:S(2)}, u32[]{:S(2)}) collective-permute-start(bf16[8,16,256]{2,1,0:T(8,128)(2,1)S(1)} %constant_dynamic-update-slice_fusion.had_ref), channel_id=1, source_target_pairs={{0,1},{1,0},{2,3},{3,2},{4,5},{5,4},{6,7},{7,6},{8,9},{9,8},{10,11... | collective-permute-start | bytes 196616 | tf_op jit(solution)/shard_map/ppermute | solution.py:124

commit v7 on v6

--- a/solution.py
+++ b/solution.py
@@ -160,17 +160,16 @@
             for index, (frame, (_, half)) in enumerate(held.items()):
                 kept[frame ^ mask] = (value[index * count:(index + 1) * count], 1 - half)
         held = kept
-    order = sorted(held)
-    return jnp.concatenate([held[frame][0] for frame in order], 0), [held[frame][1] for frame in order]
-
-
-def power_kernel(taps, groups, scale, halves, had_ref, got_ref, out_hbm, terms, made, sems):
+    return jnp.concatenate([value for value, _ in held.values()], 0), [(frame, half) for frame, (_, half) in held.items()]
+
+
+def power_kernel(taps, groups, scale, order, had_ref, got_ref, out_hbm, terms, made, sems):
     frames, columns = terms.shape[1], terms.shape[3]
     per_tap = PARTS * CH_DEV
     tiles = columns // LANES
-    for frame, half in enumerate(halves):
-        terms[half, frame] = had_ref[frame]
-        terms[1 - half, frame] = got_ref[frame]
+    for position, (frame, half) in enumerate(order):
+        terms[half, frame] = had_ref[position]
+        terms[1 - half, frame] = got_ref[position]
     group = lax.axis_index("tgrp")
     mine = lax.axis_index("chan") * groups + group
     rows = 2 * columns // groups
@@ -227,13 +226,13 @@
         copy.wait()
 
 
-def powers(had, halves, taps):
+def powers(had, order, taps):
     groups = lax.axis_size("tgrp")
     frames, depth, columns = had.shape
     rows = 2 * columns // groups
     tiles = columns // LANES
     out = pl.pallas_call(
-        functools.partial(power_kernel, taps, groups, 1.0 / frames, halves),
+        functools.partial(power_kernel, taps, groups, 1.0 / frames, order),
         out_shape=jax.ShapeDtypeStruct((rows * CH_DEV * tiles * PARTS, LANES), jnp.float32),
         in_specs=[pl.BlockSpec(memory_space=pltpu.VMEM)] * 2,
         out_specs=pl.BlockSpec(memory_space=pltpu.HBM),
@@ -251,8 +250,8 @@
 
 def body(voltages, filter_taps):
     terms = transform(voltages[0], filter_taps)
-    had, halves = exchanged(terms)
-    return powers(had, halves, filter_taps.shape[0])
+    had, order = exchanged(terms)
+    return powers(had, order, filter_taps.shape[0])
 
 
 def solution(mesh):

time: 16.8 us -> 16.8 us (level)
  no operation moved by 1% of the time
where the time goes in v7:
time: 16.8 us; the launch traced here: 16.6 us
  starting transfers between devices  8.69 us (52%)
  Pallas kernels  4.08 us (24%)
  waiting for transfers between devices  3.78 us (22%)
    ppermute x5, starting transfers between devices, moved(): lax.ppermute(array, AXES, [(i, i ^ masks[i % 2] * 2 + 1) for i in range(d...  8.69 us
    ppermute x5, waiting for transfers between devices, moved(): lax.ppermute(array, AXES, [(i, i ^ masks[i % 2] * 2 + 1) for i in range(d...  3.78 us
    pallas_call x1, Pallas kernels, transform(): pl.pallas_call(functools.partial(transform_kernel, chunk), out_shape=jax....  2.81 us
    pallas_call x1, Pallas kernels, powers(): pl.pallas_call(functools.partial(power_kernel, taps, groups, 1.0 / frames...  1.27 us
  transfers between devices with their start and end apart: 5, of which 4 were waited for; matrix products, arithmetic and copies ran while one was open for 0% of the time, Pallas kernels for 0%

profile of v7, /device:TPU:0, one launch (start us, length us, event | category | flops | bytes accessed | tf_op | source)
XLA Modules:
  0.0 16.6 jit_solution(16795720319082813275)
XLA Ops:
  0.0 2.8 %transform.1 = bf16[4,16,256]{2,1,0:T(8,128)(2,1)S(1)} custom-call(bf16[8192,256]{1,0:T(8,128)(2,1)} %bitcast.6, f32[4,8192]{1,0:T(4,128)} %taps_hbm.1, f32[16,2176]{1,0:T(8,128)} %constant.8.clone.twiddle_hbm), custom_call_target="tpu_custom_call" | custom-call | tf_op jit(solution)/shard_map/transform/pallas_call | solution.py:105
  2.8 3.5 %collective-permute-start = (bf16[2,16,256]{2,1,0:T(8,128)(2,1)S(1)}, bf16[2,16,256]{2,1,0:T(8,128)(2,1)S(1)}, u32[]{:S(2)}, u32[]{:S(2)}) collective-permute-start(bf16[2,16,256]{2,1,0:T(8,128)(2,1)S(1)} %slice.37), channel_id=1, source_target_pairs={{0,9},{1,8},{2,11},{3,10},{4,13},{5,12},{6,15},{7,14},{8,1},{9,0},... | collective-permute-start | bytes 49160 | tf_op jit(solution)/shard_map/ppermute | solution.py:124
  6.4 1.4 %collective-permute-done = bf16[2,16,256]{2,1,0:T(8,128)(2,1)S(1)} collective-permute-done((bf16[2,16,256]{2,1,0:T(8,128)(2,1)S(1)}, bf16[2,16,256]{2,1,0:T(8,128)(2,1)S(1)}, u32[]{:S(2)}, u32[]{:S(2)}) %collective-permute-start) | collective-permute-done | bytes 16416 | tf_op jit(solution)/shard_map/ppermute | solution.py:124
  7.8 1.9 %collective-permute-start.2 = (bf16[2,16,256]{2,1,0:T(8,128)(2,1)S(1)}, bf16[2,16,256]{2,1,0:T(8,128)(2,1)S(1)}, u32[]{:S(2)}, u32[]{:S(2)}) collective-permute-start(bf16[2,16,256]{2,1,0:T(8,128)(2,1)S(1)} %get-tuple-element.5), channel_id=1, source_target_pairs={{0,3},{1,4},{2,1},{3,6},{4,7},{5,0},{6,5},{7,2},{8,11},{9,12},{10,... | collective-permute-start | bytes 49160 | tf_op jit(solution)/shard_map/ppermute | solution.py:124
  9.7 0.2 collective-permute-start.1
  9.8 2.6 %collective-permute-start.3 = (bf16[2,16,256]{2,1,0:T(8,128)(2,1)S(1)}, bf16[2,16,256]{2,1,0:T(8,128)(2,1)S(1)}, u32[]{:S(2)}, u32[]{:S(2)}) collective-permute-start(bf16[2,16,256]{2,1,0:T(8,128)(2,1)S(1)} %get-tuple-element.10), channel_id=1, source_target_pairs={{0,7},{1,6},{2,5},{3,4},{4,3},{5,2},{6,1},{7,0},{8,15},{9,14},{10,... | collective-permute-start | bytes 49160 | tf_op jit(solution)/shard_map/ppermute | solution.py:124
  12.4 0.0 collective-permute-done.2
  12.4 0.4 %collective-permute-done.1 = bf16[2,16,256]{2,1,0:T(8,128)(2,1)S(1)} collective-permute-done((bf16[2,16,256]{2,1,0:T(8,128)(2,1)S(1)}, bf16[2,16,256]{2,1,0:T(8,128)(2,1)S(1)}, u32[]{:S(2)}, u32[]{:S(2)}) %collective-permute-start.1) | collective-permute-done | bytes 16416 | tf_op jit(solution)/shard_map/ppermute | solution.py:124
  12.9 1.0 %collective-permute-done.3 = bf16[2,16,256]{2,1,0:T(8,128)(2,1)S(1)} collective-permute-done((bf16[2,16,256]{2,1,0:T(8,128)(2,1)S(1)}, bf16[2,16,256]{2,1,0:T(8,128)(2,1)S(1)}, u32[]{:S(2)}, u32[]{:S(2)}) %collective-permute-start.3) | collective-permute-done | bytes 16416 | tf_op jit(solution)/shard_map/ppermute | solution.py:124
  13.9 0.5 %collective-permute-start.4 = (bf16[8,16,256]{2,1,0:T(8,128)(2,1)S(1)}, bf16[8,16,256]{2,1,0:T(8,128)(2,1)S(1)}, u32[]{:S(2)}, u32[]{:S(2)}) collective-permute-start(bf16[8,16,256]{2,1,0:T(8,128)(2,1)S(1)} %constant_dynamic-update-slice_fusion.had_ref), channel_id=1, source_target_pairs={{0,1},{1,0},{2,3},{3,2},{4,5},{5,4},{6,7},{7,6},{8,9},{9,8},{10,11... | collective-permute-start | bytes 196616 | tf_op jit(solution)/shard_map/ppermute | solution.py:124
  14.4 0.9 %collective-permute-done.4.got_ref = bf16[8,16,256]{2,1,0:T(8,128)(2,1)S(1)} collective-permute-done((bf16[8,16,256]{2,1,0:T(8,128)(2,1)S(1)}, bf16[8,16,256]{2,1,0:T(8,128)(2,1)S(1)}, u32[]{:S(2)}, u32[]{:S(2)}) %collective-permute-start.4) | collective-permute-done | bytes 65568 | tf_op jit(solution)/shard_map/ppermute | solution.py:124
  15.3 1.3 %powers.1 = f32[2048,128]{1,0:T(8,128)} custom-call(bf16[8,16,256]{2,1,0:T(8,128)(2,1)S(1)} %constant_dynamic-update-slice_fusion.had_ref, bf16[8,16,256]{2,1,0:T(8,128)(2,1)S(1)} %collective-permute-done.4.got_ref), custom_call_target="tpu_custom_call" | custom-call | tf_op jit(solution)/shard_map/powers/pallas_call | solution.py:234
  (7 shorter events, 0.0 us)
Async XLA Ops:
  2.8 5.0 %collective-permute-start = (bf16[2,16,256]{2,1,0:T(8,128)(2,1)S(1)}, bf16[2,16,256]{2,1,0:T(8,128)(2,1)S(1)}, u32[]{:S(2)}, u32[]{:S(2)}) collective-permute-start(bf16[2,16,256]{2,1,0:T(8,128)(2,1)S(1)} %slice.37), channel_id=1, source_target_pairs={{0,9},{1,8},{2,11},{3,10},{4,13},{5,12},{6,15},{7,14},{8,1},{9,0},... | collective-permute-start | bytes 49160 | tf_op jit(solution)/shard_map/ppermute | solution.py:124
  7.8 4.6 %collective-permute-start.2 = (bf16[2,16,256]{2,1,0:T(8,128)(2,1)S(1)}, bf16[2,16,256]{2,1,0:T(8,128)(2,1)S(1)}, u32[]{:S(2)}, u32[]{:S(2)}) collective-permute-start(bf16[2,16,256]{2,1,0:T(8,128)(2,1)S(1)} %get-tuple-element.5), channel_id=1, source_target_pairs={{0,3},{1,4},{2,1},{3,6},{4,7},{5,0},{6,5},{7,2},{8,11},{9,12},{10,... | collective-permute-start | bytes 49160 | tf_op jit(solution)/shard_map/ppermute | solution.py:124
  9.7 3.2 %collective-permute-start.1 = (bf16[2,16,256]{2,1,0:T(8,128)(2,1)S(1)}, bf16[2,16,256]{2,1,0:T(8,128)(2,1)S(1)}, u32[]{:S(2)}, u32[]{:S(2)}) collective-permute-start(bf16[2,16,256]{2,1,0:T(8,128)(2,1)S(1)} %get-tuple-element.6), channel_id=1, source_target_pairs={{0,5},{1,2},{2,7},{3,0},{4,1},{5,6},{6,3},{7,4},{8,13},{9,10},{10,... | collective-permute-start | bytes 49160 | tf_op jit(solution)/shard_map/ppermute | solution.py:124
  9.8 4.1 %collective-permute-start.3 = (bf16[2,16,256]{2,1,0:T(8,128)(2,1)S(1)}, bf16[2,16,256]{2,1,0:T(8,128)(2,1)S(1)}, u32[]{:S(2)}, u32[]{:S(2)}) collective-permute-start(bf16[2,16,256]{2,1,0:T(8,128)(2,1)S(1)} %get-tuple-element.10), channel_id=1, source_target_pairs={{0,7},{1,6},{2,5},{3,4},{4,3},{5,2},{6,1},{7,0},{8,15},{9,14},{10,... | collective-permute-start | bytes 49160 | tf_op jit(solution)/shard_map/ppermute | solution.py:124
  13.9 1.4 %collective-permute-start.4 = (bf16[8,16,256]{2,1,0:T(8,128)(2,1)S(1)}, bf16[8,16,256]{2,1,0:T(8,128)(2,1)S(1)}, u32[]{:S(2)}, u32[]{:S(2)}) collective-permute-start(bf16[8,16,256]{2,1,0:T(8,128)(2,1)S(1)} %constant_dynamic-update-slice_fusion.had_ref), channel_id=1, source_target_pairs={{0,1},{1,0},{2,3},{3,2},{4,5},{5,4},{6,7},{7,6},{8,9},{9,8},{10,11... | collective-permute-start | bytes 196616 | tf_op jit(solution)/shard_map/ppermute | solution.py:124

commit v8 on v7

--- a/solution.py
+++ b/solution.py
@@ -207,16 +207,18 @@
     ).astype(jnp.bfloat16)
     left = left.astype(jnp.bfloat16)
     per_row = CH_DEV * tiles * PARTS
-    part_rows = max(rows // WRITES, 8)
+    shares = [rows // 8, rows // 4, rows // 4, rows - rows // 8 - rows // 2]
+    at = 0
     copies = []
-    for step in range(rows // part_rows):
+    for step, part_rows in enumerate(shares):
         product = scale * lax.dot_general(
-            left[:, step * part_rows:(step + 1) * part_rows],
+            left[:, at:at + part_rows],
             against,
             (((0,), (0,)), ((), ())),
             preferred_element_type=jnp.float32,
         )
-        start = step * part_rows * per_row
+        start = at * per_row
+        at += part_rows
         for index in range(per_row):
             made[pl.ds(start + index, part_rows, stride=per_row), :] = product[:, index * LANES:(index + 1) * LANES]
         span = pl.ds(start, part_rows * per_row)

time: 16.8 us -> 16.8 us (level)
  no operation moved by 1% of the time
where the time goes in v8:
time: 16.8 us; the launch traced here: 16.6 us
  starting transfers between devices  8.69 us (52%)
  Pallas kernels  4.1 us (24%)
  waiting for transfers between devices  3.78 us (22%)
    ppermute x5, starting transfers between devices, moved(): lax.ppermute(array, AXES, [(i, i ^ masks[i % 2] * 2 + 1) for i in range(d...  8.69 us
    ppermute x5, waiting for transfers between devices, moved(): lax.ppermute(array, AXES, [(i, i ^ masks[i % 2] * 2 + 1) for i in range(d...  3.78 us
    pallas_call x1, Pallas kernels, transform(): pl.pallas_call(functools.partial(transform_kernel, chunk), out_shape=jax....  2.81 us
    pallas_call x1, Pallas kernels, powers(): pl.pallas_call(functools.partial(power_kernel, taps, groups, 1.0 / frames...  1.29 us
  transfers between devices with their start and end apart: 5, of which 4 were waited for; matrix products, arithmetic and copies ran while one was open for 0% of the time, Pallas kernels for 0%

profile of v8, /device:TPU:0, one launch (start us, length us, event | category | flops | bytes accessed | tf_op | source)
XLA Modules:
  0.0 16.6 jit_solution(2823600209332381532)
XLA Ops:
  0.0 2.8 %transform.1 = bf16[4,16,256]{2,1,0:T(8,128)(2,1)S(1)} custom-call(bf16[8192,256]{1,0:T(8,128)(2,1)} %bitcast.6, f32[4,8192]{1,0:T(4,128)} %taps_hbm.1, f32[16,2176]{1,0:T(8,128)} %constant.8.clone.twiddle_hbm), custom_call_target="tpu_custom_call" | custom-call | tf_op jit(solution)/shard_map/transform/pallas_call | solution.py:105
  2.8 3.5 %collective-permute-start = (bf16[2,16,256]{2,1,0:T(8,128)(2,1)S(1)}, bf16[2,16,256]{2,1,0:T(8,128)(2,1)S(1)}, u32[]{:S(2)}, u32[]{:S(2)}) collective-permute-start(bf16[2,16,256]{2,1,0:T(8,128)(2,1)S(1)} %slice.37), channel_id=1, source_target_pairs={{0,9},{1,8},{2,11},{3,10},{4,13},{5,12},{6,15},{7,14},{8,1},{9,0},... | collective-permute-start | bytes 49160 | tf_op jit(solution)/shard_map/ppermute | solution.py:124
  6.4 1.4 %collective-permute-done = bf16[2,16,256]{2,1,0:T(8,128)(2,1)S(1)} collective-permute-done((bf16[2,16,256]{2,1,0:T(8,128)(2,1)S(1)}, bf16[2,16,256]{2,1,0:T(8,128)(2,1)S(1)}, u32[]{:S(2)}, u32[]{:S(2)}) %collective-permute-start) | collective-permute-done | bytes 16416 | tf_op jit(solution)/shard_map/ppermute | solution.py:124
  7.8 1.9 %collective-permute-start.2 = (bf16[2,16,256]{2,1,0:T(8,128)(2,1)S(1)}, bf16[2,16,256]{2,1,0:T(8,128)(2,1)S(1)}, u32[]{:S(2)}, u32[]{:S(2)}) collective-permute-start(bf16[2,16,256]{2,1,0:T(8,128)(2,1)S(1)} %get-tuple-element.5), channel_id=1, source_target_pairs={{0,3},{1,4},{2,1},{3,6},{4,7},{5,0},{6,5},{7,2},{8,11},{9,12},{10,... | collective-permute-start | bytes 49160 | tf_op jit(solution)/shard_map/ppermute | solution.py:124
  9.7 0.2 collective-permute-start.1
  9.8 2.6 %collective-permute-start.3 = (bf16[2,16,256]{2,1,0:T(8,128)(2,1)S(1)}, bf16[2,16,256]{2,1,0:T(8,128)(2,1)S(1)}, u32[]{:S(2)}, u32[]{:S(2)}) collective-permute-start(bf16[2,16,256]{2,1,0:T(8,128)(2,1)S(1)} %get-tuple-element.10), channel_id=1, source_target_pairs={{0,7},{1,6},{2,5},{3,4},{4,3},{5,2},{6,1},{7,0},{8,15},{9,14},{10,... | collective-permute-start | bytes 49160 | tf_op jit(solution)/shard_map/ppermute | solution.py:124
  12.4 0.0 collective-permute-done.2
  12.4 0.4 %collective-permute-done.1 = bf16[2,16,256]{2,1,0:T(8,128)(2,1)S(1)} collective-permute-done((bf16[2,16,256]{2,1,0:T(8,128)(2,1)S(1)}, bf16[2,16,256]{2,1,0:T(8,128)(2,1)S(1)}, u32[]{:S(2)}, u32[]{:S(2)}) %collective-permute-start.1) | collective-permute-done | bytes 16416 | tf_op jit(solution)/shard_map/ppermute | solution.py:124
  12.9 1.0 %collective-permute-done.3 = bf16[2,16,256]{2,1,0:T(8,128)(2,1)S(1)} collective-permute-done((bf16[2,16,256]{2,1,0:T(8,128)(2,1)S(1)}, bf16[2,16,256]{2,1,0:T(8,128)(2,1)S(1)}, u32[]{:S(2)}, u32[]{:S(2)}) %collective-permute-start.3) | collective-permute-done | bytes 16416 | tf_op jit(solution)/shard_map/ppermute | solution.py:124
  13.9 0.5 %collective-permute-start.4 = (bf16[8,16,256]{2,1,0:T(8,128)(2,1)S(1)}, bf16[8,16,256]{2,1,0:T(8,128)(2,1)S(1)}, u32[]{:S(2)}, u32[]{:S(2)}) collective-permute-start(bf16[8,16,256]{2,1,0:T(8,128)(2,1)S(1)} %constant_dynamic-update-slice_fusion.had_ref), channel_id=1, source_target_pairs={{0,1},{1,0},{2,3},{3,2},{4,5},{5,4},{6,7},{7,6},{8,9},{9,8},{10,11... | collective-permute-start | bytes 196616 | tf_op jit(solution)/shard_map/ppermute | solution.py:124
  14.4 0.9 %collective-permute-done.4.got_ref = bf16[8,16,256]{2,1,0:T(8,128)(2,1)S(1)} collective-permute-done((bf16[8,16,256]{2,1,0:T(8,128)(2,1)S(1)}, bf16[8,16,256]{2,1,0:T(8,128)(2,1)S(1)}, u32[]{:S(2)}, u32[]{:S(2)}) %collective-permute-start.4) | collective-permute-done | bytes 65568 | tf_op jit(solution)/shard_map/ppermute | solution.py:124
  15.3 1.3 %powers.1 = f32[2048,128]{1,0:T(8,128)} custom-call(bf16[8,16,256]{2,1,0:T(8,128)(2,1)S(1)} %constant_dynamic-update-slice_fusion.had_ref, bf16[8,16,256]{2,1,0:T(8,128)(2,1)S(1)} %collective-permute-done.4.got_ref), custom_call_target="tpu_custom_call" | custom-call | tf_op jit(solution)/shard_map/powers/pallas_call | solution.py:236
  (7 shorter events, 0.0 us)
Async XLA Ops:
  2.8 5.0 %collective-permute-start = (bf16[2,16,256]{2,1,0:T(8,128)(2,1)S(1)}, bf16[2,16,256]{2,1,0:T(8,128)(2,1)S(1)}, u32[]{:S(2)}, u32[]{:S(2)}) collective-permute-start(bf16[2,16,256]{2,1,0:T(8,128)(2,1)S(1)} %slice.37), channel_id=1, source_target_pairs={{0,9},{1,8},{2,11},{3,10},{4,13},{5,12},{6,15},{7,14},{8,1},{9,0},... | collective-permute-start | bytes 49160 | tf_op jit(solution)/shard_map/ppermute | solution.py:124
  7.8 4.6 %collective-permute-start.2 = (bf16[2,16,256]{2,1,0:T(8,128)(2,1)S(1)}, bf16[2,16,256]{2,1,0:T(8,128)(2,1)S(1)}, u32[]{:S(2)}, u32[]{:S(2)}) collective-permute-start(bf16[2,16,256]{2,1,0:T(8,128)(2,1)S(1)} %get-tuple-element.5), channel_id=1, source_target_pairs={{0,3},{1,4},{2,1},{3,6},{4,7},{5,0},{6,5},{7,2},{8,11},{9,12},{10,... | collective-permute-start | bytes 49160 | tf_op jit(solution)/shard_map/ppermute | solution.py:124
  9.7 3.2 %collective-permute-start.1 = (bf16[2,16,256]{2,1,0:T(8,128)(2,1)S(1)}, bf16[2,16,256]{2,1,0:T(8,128)(2,1)S(1)}, u32[]{:S(2)}, u32[]{:S(2)}) collective-permute-start(bf16[2,16,256]{2,1,0:T(8,128)(2,1)S(1)} %get-tuple-element.6), channel_id=1, source_target_pairs={{0,5},{1,2},{2,7},{3,0},{4,1},{5,6},{6,3},{7,4},{8,13},{9,10},{10,... | collective-permute-start | bytes 49160 | tf_op jit(solution)/shard_map/ppermute | solution.py:124
  9.8 4.1 %collective-permute-start.3 = (bf16[2,16,256]{2,1,0:T(8,128)(2,1)S(1)}, bf16[2,16,256]{2,1,0:T(8,128)(2,1)S(1)}, u32[]{:S(2)}, u32[]{:S(2)}) collective-permute-start(bf16[2,16,256]{2,1,0:T(8,128)(2,1)S(1)} %get-tuple-element.10), channel_id=1, source_target_pairs={{0,7},{1,6},{2,5},{3,4},{4,3},{5,2},{6,1},{7,0},{8,15},{9,14},{10,... | collective-permute-start | bytes 49160 | tf_op jit(solution)/shard_map/ppermute | solution.py:124
  13.9 1.4 %collective-permute-start.4 = (bf16[8,16,256]{2,1,0:T(8,128)(2,1)S(1)}, bf16[8,16,256]{2,1,0:T(8,128)(2,1)S(1)}, u32[]{:S(2)}, u32[]{:S(2)}) collective-permute-start(bf16[8,16,256]{2,1,0:T(8,128)(2,1)S(1)} %constant_dynamic-update-slice_fusion.had_ref), channel_id=1, source_target_pairs={{0,1},{1,0},{2,3},{3,2},{4,5},{5,4},{6,7},{7,6},{8,9},{9,8},{10,11... | collective-permute-start | bytes 196616 | tf_op jit(solution)/shard_map/ppermute | solution.py:124
